TPU v7x, 32 devices: a whole 2x2x4 slice. The times are simulated.
32 devices in a mesh: stream: 2 (over y), batch: 16 (over z, x, core).
Axes of the slice: x: 2, y: 2, z: 4, core: 2. Of those that a mesh axis runs over, the one named last changes fastest.
Arguments:
- layer_input: bfloat16 [2, 16, 1024, 768], P('stream', 'batch'), may hold values from -6 to 6
- out_cotangent: bfloat16 [2, 16, 1024, 768], P('stream', 'batch'), may hold values from -6 to 6
- block_size: int32 [16], P('batch'), may hold values from 4 to 16, as said below
- norm1_gain: float32 [768], replicated, may hold values from 0.5 to 1.5
- norm1_bias: float32 [768], replicated, may hold values from -1 to 1
- qkv_weight: bfloat16 [768, 2304], replicated, may hold values from -0.21875 to 0.21875
- qkv_bias: float32 [2304], replicated, may hold values from -1 to 1
- proj_weight: bfloat16 [768, 768], replicated, may hold values from -0.875 to 0.875
- proj_bias: float32 [768], replicated, may hold values from -1 to 1
- norm2_gain: float32 [768], replicated, may hold values from 0.5 to 1.5
- norm2_bias: float32 [768], replicated, may hold values from -1 to 1
- up_weight: bfloat16 [768, 3072], replicated, may hold values from -0.21875 to 0.21875
- up_bias: float32 [3072], replicated, may hold values from -1 to 1
- down_weight: bfloat16 [3072, 768], replicated, may hold values from -0.109375 to 0.109375
- down_bias: float32 [768], replicated, may hold values from -1 to 1
Outputs:
- layer_output: bfloat16 [2, 16, 1024, 768], P('stream', 'batch')
- input_grad: float32 [2, 16, 1024, 768], P('stream', 'batch')
- gain1_grad: float32 [768], P('batch')
- bias1_grad: float32 [768], P('batch')
- qkvw_grad: float32 [768, 2304], P('batch')
- qkvb_grad: float32 [2304], P('batch')
- projw_grad: float32 [768, 768], P('batch')
- projb_grad: float32 [768], P('batch')
- gain2_grad: float32 [768], P('batch')
- bias2_grad: float32 [768], P('batch')
- upw_grad: float32 [768, 3072], P('batch')
- upb_grad: float32 [3072], P('batch')
- downw_grad: float32 [3072, 768], P('batch')
- downb_grad: float32 [768], P('batch')
Inputs may be any that keep to these rules, and one draw needn't show every extreme that they name: `block_size`: each sequence's block size is 4, 8 or 16.
All inputs are finite; a program needn't handle non-finite values.
Results may differ from a plain program's by a relative error of at most 0.014.
Values may be sent and summed in bfloat16 or wider, within the bound.
No kernel may reach another device: no remote copies, remote signals or barrier semaphores. Data moves between devices by JAX's collectives and lax.ppermute only.
A program may use at most 384 MiB of HBM per device.

v0:
```python
from functools import partial
import math

import jax
import jax.numpy as jnp
from jax import lax
from jax.sharding import PartitionSpec as P

HEAD = 64
TILE = 512


masked_value = -1e30
epsilon = 1e-05
window_rows = 16


def shifted(block, axis, distance):
    devices = range(lax.axis_size(axis))
    route = [(i - distance, i) for i in devices if i - distance in devices]
    return lax.ppermute(block, axis, route)


def normalize(values):
    mean = jnp.mean(values, axis=-1, keepdims=True)
    centred = values - mean
    factor = lax.rsqrt(jnp.mean(centred * centred, axis=-1, keepdims=True) + epsilon)
    return (centred * factor, factor)


def norm_back(grad_normed, normed, factor):
    first = jnp.mean(grad_normed, axis=-1, keepdims=True)
    second = jnp.mean(grad_normed * normed, axis=-1, keepdims=True)
    return factor * (grad_normed - first - normed * second)


def rotary_tables(length, width):
    places = jnp.arange(length, dtype=jnp.float32)[:, None]
    column = jnp.arange(width, dtype=jnp.int32) % HEAD
    index = (column % (HEAD // 2)).astype(jnp.float32)
    angle = places * jnp.exp(index * (-2.0 * math.log(10000.0) / HEAD))[None, :]
    return (jnp.cos(angle), jnp.sin(angle))


def turn(values):
    shape = values.shape
    split = values.reshape(shape[:-1] + (shape[-1] // HEAD, 2, HEAD // 2))
    return jnp.concatenate((-split[..., 1:, :], split[..., :1, :]), axis=-2).reshape(shape)


def turn_back(values):
    shape = values.shape
    split = values.reshape(shape[:-1] + (shape[-1] // HEAD, 2, HEAD // 2))
    return jnp.concatenate((split[..., 1:, :], -split[..., :1, :]), axis=-2).reshape(shape)


def head_view(values):
    return values.reshape(values.shape[0], values.shape[1] // HEAD, HEAD)


def window_view(values):
    return values.reshape(
        values.shape[0] // window_rows, window_rows, values.shape[1] // HEAD, HEAD
    )


def scores_of(query, keys, allowed):
    raw = jnp.einsum(
        "qhd,khd->hqk", head_view(query), head_view(keys), preferred_element_type=jnp.float32
    )
    return jnp.where(allowed[None], raw * (1.0 / math.sqrt(HEAD)), masked_value)


def window_scores(query, keys, rows):
    groups = rows.reshape(-1, window_rows)
    allowed = groups[:, :, None] == groups[:, None, :]
    raw = jnp.einsum(
        "gqhd,gkhd->hgqk", window_view(query), window_view(keys), preferred_element_type=jnp.float32
    )
    return jnp.where(allowed[None], raw * (1.0 / math.sqrt(HEAD)), masked_value)


def clean_forward(query, keys, values, allowed):
    scores = scores_of(query, keys, allowed)
    top = jnp.max(scores, axis=-1)
    log_total = top + jnp.log(jnp.sum(jnp.exp(scores - top[..., None]), axis=-1))
    mixed = jnp.einsum(
        "hqk,khd->qhd",
        jnp.exp(scores - log_total[..., None]).astype(jnp.bfloat16),
        head_view(values),
        preferred_element_type=jnp.float32,
    )
    return (mixed.reshape(query.shape[0], query.shape[1]), log_total)


def noisy_forward(query, keys, values, far_keys, far_values, rows, allowed):
    heads = query.shape[1] // HEAD
    far = scores_of(query, far_keys, allowed)
    near = window_scores(query, keys, rows)
    near_flat = near.reshape(heads, query.shape[0], window_rows)
    top = jnp.maximum(jnp.max(far, axis=-1), jnp.max(near_flat, axis=-1))
    total = jnp.sum(jnp.exp(far - top[..., None]), axis=-1) + jnp.sum(
        jnp.exp(near_flat - top[..., None]), axis=-1
    )
    log_total = top + jnp.log(total)
    log_window = log_total.reshape(heads, -1, window_rows)
    far_mix = jnp.einsum(
        "hqk,khd->qhd",
        jnp.exp(far - log_total[..., None]).astype(jnp.bfloat16),
        head_view(far_values),
        preferred_element_type=jnp.float32,
    )
    near_mix = jnp.einsum(
        "hgqk,gkhd->gqhd",
        jnp.exp(near - log_window[..., None]).astype(jnp.bfloat16),
        window_view(values),
        preferred_element_type=jnp.float32,
    )
    result = far_mix.reshape(query.shape[0], -1) + near_mix.reshape(query.shape[0], -1)
    return (result, log_total)


def clean_backward(query, grad_out, log_total, keys, values, allowed):
    factor = 1.0 / math.sqrt(HEAD)
    prob = jnp.exp(scores_of(query, keys, allowed) - log_total[..., None])
    dprob = jnp.einsum(
        "qhd,khd->hqk", head_view(grad_out), head_view(values), preferred_element_type=jnp.float32
    )
    delta = jnp.sum(prob * dprob, axis=-1)
    dscore = (prob * (dprob - delta[..., None])).astype(jnp.bfloat16)
    grad_query = jnp.einsum(
        "hqk,khd->qhd", dscore, head_view(keys), preferred_element_type=jnp.float32
    )
    grad_key = (
        jnp.einsum("hqk,qhd->khd", dscore, head_view(query), preferred_element_type=jnp.float32)
        * factor
    )
    grad_value = jnp.einsum(
        "hqk,qhd->khd",
        prob.astype(jnp.bfloat16),
        head_view(grad_out),
        preferred_element_type=jnp.float32,
    )
    return (
        (grad_query * factor).reshape(query.shape[0], -1),
        grad_key.reshape(keys.shape[0], -1),
        grad_value.reshape(keys.shape[0], -1),
    )


def noisy_backward(query, grad_out, log_total, keys, values, far_keys, far_values, rows, allowed):
    factor = 1.0 / math.sqrt(HEAD)
    heads = query.shape[1] // HEAD
    count = query.shape[0]
    log_window = log_total.reshape(heads, -1, window_rows)
    far_prob = jnp.exp(scores_of(query, far_keys, allowed) - log_total[..., None])
    near_prob = jnp.exp(window_scores(query, keys, rows) - log_window[..., None])
    far_dprob = jnp.einsum(
        "qhd,khd->hqk",
        head_view(grad_out),
        head_view(far_values),
        preferred_element_type=jnp.float32,
    )
    near_dprob = jnp.einsum(
        "gqhd,gkhd->hgqk",
        window_view(grad_out),
        window_view(values),
        preferred_element_type=jnp.float32,
    )
    delta = jnp.sum(far_prob * far_dprob, axis=-1) + jnp.sum(
        near_prob * near_dprob, axis=-1
    ).reshape(heads, count)
    far_dscore = (far_prob * (far_dprob - delta[..., None])).astype(jnp.bfloat16)
    near_dscore = (
        near_prob * (near_dprob - delta.reshape(heads, -1, window_rows)[..., None])
    ).astype(jnp.bfloat16)
    grad_query = jnp.einsum(
        "hqk,khd->qhd", far_dscore, head_view(far_keys), preferred_element_type=jnp.float32
    ).reshape(count, -1) + jnp.einsum(
        "hgqk,gkhd->gqhd", near_dscore, window_view(keys), preferred_element_type=jnp.float32
    ).reshape(
        count, -1
    )
    far_gk = (
        jnp.einsum("hqk,qhd->khd", far_dscore, head_view(query), preferred_element_type=jnp.float32)
        * factor
    )
    far_gv = jnp.einsum(
        "hqk,qhd->khd",
        far_prob.astype(jnp.bfloat16),
        head_view(grad_out),
        preferred_element_type=jnp.float32,
    )
    near_gk = (
        jnp.einsum(
            "hgqk,gqhd->gkhd", near_dscore, window_view(query), preferred_element_type=jnp.float32
        )
        * factor
    )
    near_gv = jnp.einsum(
        "hgqk,gqhd->gkhd",
        near_prob.astype(jnp.bfloat16),
        window_view(grad_out),
        preferred_element_type=jnp.float32,
    )
    return (
        grad_query * factor,
        near_gk.reshape(count, -1),
        near_gv.reshape(count, -1),
        far_gk.reshape(far_keys.shape[0], -1),
        far_gv.reshape(far_keys.shape[0], -1),
    )


def sequence_forward(items, noisy):
    query, keys, values, far_keys, far_values, size = items
    length = query.shape[0]
    blocks = jnp.arange(length, dtype=jnp.int32) // size
    outputs = []
    totals = []
    for tile in range(length // TILE):
        start = tile * TILE
        stop = start + TILE
        rows = blocks[start:stop]
        query_part = query[start:stop]

        def clean_side(operand):
            return clean_forward(
                query_part, keys[:stop], values[:stop], rows[:, None] >= blocks[None, :stop]
            )

        def noisy_side(operand):
            return noisy_forward(
                query_part,
                keys[start:stop],
                values[start:stop],
                far_keys[:stop],
                far_values[:stop],
                rows,
                rows[:, None] > blocks[None, :stop],
            )

        piece, piece_total = lax.cond(noisy, noisy_side, clean_side, 0)
        outputs.append(piece)
        totals.append(piece_total)
    return (jnp.concatenate(outputs, axis=0), jnp.concatenate(totals, axis=1))


def sequence_backward(items, noisy):
    query, keys, values, far_keys, far_values, size, grad_out, log_total = items
    length, width = query.shape
    blocks = jnp.arange(length, dtype=jnp.int32) // size
    grad_queries = []
    grad_keys = jnp.zeros((length, width), jnp.float32)
    grad_values = jnp.zeros((length, width), jnp.float32)
    grad_far_keys = jnp.zeros((length, width), jnp.float32)
    grad_far_values = jnp.zeros((length, width), jnp.float32)
    for tile in range(length // TILE):
        start = tile * TILE
        stop = start + TILE
        rows = blocks[start:stop]
        query_part = query[start:stop]
        grad_part = grad_out[start:stop]
        total_part = log_total[:, start:stop]

        def clean_side(operand):
            grad_q, part_k, part_v = clean_backward(
                query_part,
                grad_part,
                total_part,
                keys[:stop],
                values[:stop],
                rows[:, None] >= blocks[None, :stop],
            )
            empty = jnp.zeros((stop, width), jnp.float32)
            return (grad_q, part_k, part_v, empty, empty)

        def noisy_side(operand):
            grad_q, near_k, near_v, far_k, far_v = noisy_backward(
                query_part,
                grad_part,
                total_part,
                keys[start:stop],
                values[start:stop],
                far_keys[:stop],
                far_values[:stop],
                rows,
                rows[:, None] > blocks[None, :stop],
            )
            own_keys = jnp.pad(near_k, ((start, 0), (0, 0)))
            own_values = jnp.pad(near_v, ((start, 0), (0, 0)))
            return (grad_q, own_keys, own_values, far_k, far_v)

        grad_q, part_k, part_v, part_fk, part_fv = lax.cond(noisy, noisy_side, clean_side, 0)
        grad_queries.append(grad_q)
        grad_keys = grad_keys.at[:stop].add(part_k)
        grad_values = grad_values.at[:stop].add(part_v)
        grad_far_keys = grad_far_keys.at[:stop].add(part_fk)
        grad_far_values = grad_far_values.at[:stop].add(part_fv)
    return (
        jnp.concatenate(grad_queries, axis=0),
        grad_keys,
        grad_values,
        grad_far_keys,
        grad_far_values,
    )


def outer(left, right):
    return lax.dot_general(
        left, right, (((0,), (0,)), ((), ())), preferred_element_type=jnp.float32
    )


def times_transpose(left, right):
    return lax.dot_general(
        left, right, (((1,), (1,)), ((), ())), preferred_element_type=jnp.float32
    )


def local(
    layer_input,
    out_cotangent,
    block_size,
    norm1_gain,
    norm1_bias,
    qkv_weight,
    qkv_bias,
    proj_weight,
    proj_bias,
    norm2_gain,
    norm2_bias,
    up_weight,
    up_bias,
    down_weight,
    down_bias,
):
    seqs = layer_input.shape[1]
    length = layer_input.shape[2]
    width = layer_input.shape[3]
    count = seqs * length
    noisy = lax.axis_index("stream") == 1
    inputs = layer_input.reshape(count, width).astype(jnp.float32)
    normed1, factor1 = normalize(inputs)
    hidden1 = (normed1 * norm1_gain + norm1_bias).astype(jnp.bfloat16)
    mixed = (jnp.dot(hidden1, qkv_weight, preferred_element_type=jnp.float32) + qkv_bias).reshape(
        seqs, length, 3 * width
    )
    cosine, sine = rotary_tables(length, width)
    raw_queries = mixed[..., :width]
    raw_keys = mixed[..., width : 2 * width]
    queries = (raw_queries * cosine + turn(raw_queries) * sine).astype(jnp.bfloat16)
    keys = (raw_keys * cosine + turn(raw_keys) * sine).astype(jnp.bfloat16)
    values = mixed[..., 2 * width :].astype(jnp.bfloat16)
    far_keys, far_values = shifted((keys, values), "stream", 1)
    attended, log_totals = lax.map(
        partial(sequence_forward, noisy=noisy),
        (queries, keys, values, far_keys, far_values, block_size),
    )
    attended_low = attended.reshape(count, width).astype(jnp.bfloat16)
    middle = (
        inputs + jnp.dot(attended_low, proj_weight, preferred_element_type=jnp.float32) + proj_bias
    )
    normed2, factor2 = normalize(middle)
    hidden2 = (normed2 * norm2_gain + norm2_bias).astype(jnp.bfloat16)
    upward = jnp.dot(hidden2, up_weight, preferred_element_type=jnp.float32) + up_bias
    active_low = jax.nn.gelu(upward).astype(jnp.bfloat16)
    result = (
        middle + jnp.dot(active_low, down_weight, preferred_element_type=jnp.float32) + down_bias
    )
    layer_output = result.astype(jnp.bfloat16).reshape(layer_input.shape)
    grad_rows = out_cotangent.reshape(count, width)
    grad_rows_wide = grad_rows.astype(jnp.float32)
    downw_grad = outer(active_low, grad_rows)
    downb_grad = jnp.sum(grad_rows_wide, axis=0)
    grad_active = times_transpose(grad_rows, down_weight)
    unused, gelu_pull = jax.vjp(jax.nn.gelu, upward)
    grad_upward = gelu_pull(grad_active)[0]
    grad_upward_low = grad_upward.astype(jnp.bfloat16)
    upw_grad = outer(hidden2, grad_upward_low)
    upb_grad = jnp.sum(grad_upward, axis=0)
    grad_hidden2 = times_transpose(grad_upward_low, up_weight)
    gain2_grad = jnp.sum(grad_hidden2 * normed2, axis=0)
    bias2_grad = jnp.sum(grad_hidden2, axis=0)
    grad_middle = grad_rows_wide + norm_back(grad_hidden2 * norm2_gain, normed2, factor2)
    projb_grad = jnp.sum(grad_middle, axis=0)
    grad_middle_low = grad_middle.astype(jnp.bfloat16)
    projw_grad = outer(attended_low, grad_middle_low)
    grad_attended = (
        times_transpose(grad_middle_low, proj_weight)
        .astype(jnp.bfloat16)
        .reshape(seqs, length, width)
    )
    grad_q, grad_k, grad_v, grad_far_k, grad_far_v = lax.map(
        partial(sequence_backward, noisy=noisy),
        (queries, keys, values, far_keys, far_values, block_size, grad_attended, log_totals),
    )
    back_keys, back_values = (
        shifted(grad_far_k.astype(jnp.bfloat16), "stream", -1).astype(grad_far_k.dtype),
        shifted(grad_far_v.astype(jnp.bfloat16), "stream", -1).astype(grad_far_v.dtype),
    )
    grad_k = grad_k + back_keys
    grad_v = grad_v + back_values
    grad_q_raw = grad_q * cosine + turn_back(grad_q * sine)
    grad_k_raw = grad_k * cosine + turn_back(grad_k * sine)
    grad_mixed = jnp.concatenate((grad_q_raw, grad_k_raw, grad_v), axis=-1).reshape(
        count, 3 * width
    )
    qkvb_grad = jnp.sum(grad_mixed, axis=0)
    grad_mixed_low = grad_mixed.astype(jnp.bfloat16)
    qkvw_grad = outer(hidden1, grad_mixed_low)
    grad_hidden1 = times_transpose(grad_mixed_low, qkv_weight)
    gain1_grad = jnp.sum(grad_hidden1 * normed1, axis=0)
    bias1_grad = jnp.sum(grad_hidden1, axis=0)
    input_grad = (grad_middle + norm_back(grad_hidden1 * norm1_gain, normed1, factor1)).reshape(
        layer_input.shape
    )
    all_parts = (
        lax.psum_scatter(gain1_grad, "batch", scatter_dimension=0, tiled=True),
        lax.psum_scatter(bias1_grad, "batch", scatter_dimension=0, tiled=True),
        lax.psum_scatter(qkvw_grad, "batch", scatter_dimension=0, tiled=True),
        lax.psum_scatter(qkvb_grad, "batch", scatter_dimension=0, tiled=True),
        lax.psum_scatter(projw_grad, "batch", scatter_dimension=0, tiled=True),
        lax.psum_scatter(projb_grad, "batch", scatter_dimension=0, tiled=True),
        lax.psum_scatter(gain2_grad, "batch", scatter_dimension=0, tiled=True),
        lax.psum_scatter(bias2_grad, "batch", scatter_dimension=0, tiled=True),
        lax.psum_scatter(upw_grad, "batch", scatter_dimension=0, tiled=True),
        lax.psum_scatter(upb_grad, "batch", scatter_dimension=0, tiled=True),
        lax.psum_scatter(downw_grad, "batch", scatter_dimension=0, tiled=True),
        lax.psum_scatter(downb_grad, "batch", scatter_dimension=0, tiled=True),
    )
    (
        gain1_grad,
        bias1_grad,
        qkvw_grad,
        qkvb_grad,
        projw_grad,
        projb_grad,
        gain2_grad,
        bias2_grad,
        upw_grad,
        upb_grad,
        downw_grad,
        downb_grad,
    ) = (
        lax.psum(all_parts[0].astype(jnp.bfloat16), "stream").astype(jnp.float32),
        lax.psum(all_parts[1].astype(jnp.bfloat16), "stream").astype(jnp.float32),
        lax.psum(all_parts[2].astype(jnp.bfloat16), "stream").astype(jnp.float32),
        lax.psum(all_parts[3].astype(jnp.bfloat16), "stream").astype(jnp.float32),
        lax.psum(all_parts[4].astype(jnp.bfloat16), "stream").astype(jnp.float32),
        lax.psum(all_parts[5].astype(jnp.bfloat16), "stream").astype(jnp.float32),
        lax.psum(all_parts[6].astype(jnp.bfloat16), "stream").astype(jnp.float32),
        lax.psum(all_parts[7].astype(jnp.bfloat16), "stream").astype(jnp.float32),
        lax.psum(all_parts[8].astype(jnp.bfloat16), "stream").astype(jnp.float32),
        lax.psum(all_parts[9].astype(jnp.bfloat16), "stream").astype(jnp.float32),
        lax.psum(all_parts[10].astype(jnp.bfloat16), "stream").astype(jnp.float32),
        lax.psum(all_parts[11].astype(jnp.bfloat16), "stream").astype(jnp.float32),
    )
    return (
        layer_output,
        input_grad,
        gain1_grad,
        bias1_grad,
        qkvw_grad,
        qkvb_grad,
        projw_grad,
        projb_grad,
        gain2_grad,
        bias2_grad,
        upw_grad,
        upb_grad,
        downw_grad,
        downb_grad,
    )


def solution(mesh):
    return jax.shard_map(
        local,
        mesh=mesh,
        in_specs=(
            P("stream", "batch", None, None),
            P("stream", "batch", None, None),
            P("batch"),
            P(),
            P(),
            P(),
            P(),
            P(),
            P(),
            P(),
            P(),
            P(),
            P(),
            P(),
            P(),
        ),
        out_specs=(
            P("stream", "batch", None, None),
            P("stream", "batch", None, None),
            P("batch"),
            P("batch"),
            P("batch", None),
            P("batch"),
            P("batch", None),
            P("batch"),
            P("batch"),
            P("batch"),
            P("batch", None),
            P("batch"),
            P("batch", None),
            P("batch"),
        ),
        check_vma=False,
    )
```

profile of v0, /device:TPU:0, one launch (start us, length us, event | category | flops | bytes accessed | tf_op | source)
XLA Modules:
  0.0 1251.4 jit_solution(17960181212357937824)
XLA Ops:
  14.3 4.3 add_bitcast_fusion
  24.2 3.5 copy.395
  31.7 3.6 copy.396
  35.3 3.5 copy.397
  42.9 3.5 copy.398
  46.4 14.8 %add_convert_fusion.6 = (bf16[1,1024,768]{2,1,0:T(8,128)(2,1)}, bf16[1,1024,768]{2,1,0:T(8,128)(2,1)}) fusion(f32[1,1024,768]{2,1,0:T(8,128)} %copy.398, f32[768]{0:T(1024)S(1)} %fusion.156, f32[1,1024,2304]{2,1,0:T(8,128)} %copy-done.11, f32[1,1024,768]{2,1,0:T(8,128)} %copy.396), kind=kLoop, calls=%fused_computation.221 | loop fusion | flops 7077888 | bytes 15731712 | tf_op jit(solution)/shard_map/convert_element_type | solution.py:353
  61.2 6.1 collective-permute-start
  82.7 18.4 %collective-permute-done = bf16[1,1024,768]{2,1,0:T(8,128)(2,1)} collective-permute-done((bf16[1,1024,768]{2,1,0:T(8,128)(2,1)}, bf16[1,1024,768]{2,1,0:T(8,128)(2,1)}, u32[]{:S(2)}, u32[]{:S(2)}) %collective-permute-start) | collective-permute-done | bytes 1572896 | tf_op jit(solution)/shard_map/ppermute | solution.py:21
  101.2 32.6 %collective-permute-done.1 = bf16[1,1024,768]{2,1,0:T(8,128)(2,1)} collective-permute-done((bf16[1,1024,768]{2,1,0:T(8,128)(2,1)}, bf16[1,1024,768]{2,1,0:T(8,128)(2,1)}, u32[]{:S(2)}, u32[]{:S(2)}) %collective-permute-start.1) | collective-permute-done | bytes 1572896 | tf_op jit(solution)/shard_map/ppermute | solution.py:21
  133.7 39.4 %conditional.4 = (f32[12,512]{1,0:T(8,128)}, bf16[512,768]{1,0:T(8,128)(2,1)}) conditional(s32[]{:T(128)} %convert_element_type.235, (s32[512]{0:T(512)S(1)}, s32[1024]{0:T(1024)S(1)}, bf16[512,768]{1,0:T(8,128)(2,1)}, bf16[1024,768]{1,0:T(8,128)(2,1)}, bf16[1024,768]{1,0:T(8,128)(2,1)}) %tuple.124, (s32[512]{0:T(512)S(1)}, s32[1024]{0:T(1024)S(1)}, ...), branch_computations={%region_2.5_spmd, %region_5.10_spmd} | conditional | flops 867225600 | bytes 105037864 | solution.py:243
  145.3 3.7 exponential_reduce_fusion
  154.2 8.7 fusion.3
  175.3 56.0 %conditional.5 = (f32[12,512]{1,0:T(8,128)}, bf16[512,768]{1,0:T(8,128)(2,1)}) conditional(s32[]{:T(128)} %convert_element_type.235, (s32[512]{0:T(512)S(1)}, s32[1024]{0:T(1024)S(1)}, bf16[512,768]{1,0:T(8,128)(2,1)}, bf16[1024,768]{1,0:T(8,128)(2,1)}, bf16[1024,768]{1,0:T(8,128)(2,1)}) %tuple.126, (s32[512]{0:T(512)S(1)}, s32[1024]{0:T(1024)S(1)}, ...), branch_computations={%region_10.13_spmd, %region_13.18_spmd} | conditional | flops 1707397120 | bytes 120090808 | solution.py:243
  181.3 14.4 %fusion.17 = (f32[12,512]{1,0:T(8,128)S(1)}, f32[12,512,1024]{2,1,0:T(8,128)}) fusion(pred[512,1024]{1,0:T(8,128)(4,1)} %broadcast_compare_fusion.3, bf16[512,12,64]{0,2,1:T(8,128)(2,1)} %bitcast.306, bf16[1024,12,64]{0,2,1:T(8,128)(2,1)} %bitcast.293), kind=kOutput, calls=%fused_computation.37 | convolution fusion | flops 824174592 | bytes 28073984 | tf_op jit(solution)/shard_map/while/body/eval_jaxpr/cond/branch_0_fun/qhd,khd->hqk/dot_general | solution.py:68
  195.7 11.8 exponential_reduce_fusion.3
  210.7 12.4 fusion.20
  233.6 3.9 fusion.172
  239.2 5.6 fusion.163
  244.8 18.3 %fusion.175 = (f32[3072]{0:T(1024)}, bf16[1024,3072]{1,0:T(8,128)(2,1)}) fusion(f32[1024,3072]{1,0:T(8,128)S(1)} %fusion.163, f32[3072]{0:T(1024)S(1)} %copy-done.87, bf16[3072,768]{1,0:T(8,128)(2,1)} %param.60, bf16[1,1,1024,768]{3,2,1,0:T(8,128)(2,1)S(1)} %copy-done.43), kind=kOutput, calls=%fused_computation.313 | convolution fusion | flops 4901041152 | bytes 25190400 | tf_op jit(solution)/shard_map/dot_general | solution.py:316
  263.1 10.4 fusion.174
  273.5 3.7 copy.413
  277.3 4.6 multiply_reduce_fusion.6
  281.9 3.9 fusion.164
  289.5 129.3 %conditional.7 = (f32[512,768]{1,0:T(8,128)}, f32[1024,768]{1,0:T(8,128)}, f32[1024,768]{1,0:T(8,128)}, f32[512,768]{0,1:T(8,128)}, f32[1024,768]{1,0:T(8,128)}, /*index=5*/f32[1024,768]{1,0:T(8,128)}) conditional(s32[]{:T(128)} %convert_element_type.235, (s32[512]{0:T(512)S(1)}, s32[1024]{0:T(1024)S(1)}, bf16[512,768]{1,0:T(8,128)(2,1)}, ...), branch_computations={%region_27.29_spmd, %region_29.32_spmd} | conditional | flops 4187201536 | bytes 304247040 | solution.py:294
  294.7 13.4 %fusion.177 = f32[12,512,1024]{2,1,0:T(8,128)} fusion(bf16[512,12,64]{0,2,1:T(8,128)(2,1)} %bitcast.272, bf16[1024,12,64]{0,2,1:T(8,128)(2,1)} %bitcast.266), kind=kOutput, calls=%fused_computation.316 | convolution fusion | flops 805306368 | bytes 27525120 | tf_op jit(solution)/shard_map/while/body/eval_jaxpr/cond/branch_0_fun/qhd,khd->hqk/dot_general | solution.py:68
  314.1 18.8 %multiply_reduce_fusion.3 = (f32[12,512]{1,0:T(8,128)}, f32[12,512,1024]{2,1,0:T(8,128)}) fusion(f32[12,512,1024]{2,1,0:T(8,128)} %fusion.177, f32[12,512]{1,0:T(8,128)} %get-tuple-element.407, pred[512,1024]{1,0:T(8,128)(4,1)} %broadcast_compare_fusion.9, bf16[512,12,64]{0,2,1:T(8,128)(2,1)} %bitcast.314, bf16[1024,12,64]{0,2,1:T(8,128)(2,1)} %bitcast.289), kind=kOutput, calls=%fused_computation.109 | convolution fusion | flops 836757504 | bytes 53264384 | tf_op jit(solution)/shard_map/while/body/eval_jaxpr/cond/branch_0_fun/qhd,khd->hqk/dot_general | solution.py:126
  332.9 22.6 %multiply_convert_fusion.3 = bf16[12,512,1024]{2,1,0:T(8,128)(2,1)} fusion(f32[12,512,1024]{2,1,0:T(8,128)} %get-tuple-element.849, f32[12,512,1024]{2,1,0:T(8,128)} %fusion.177, f32[12,512]{1,0:T(8,128)} %get-tuple-element.848, f32[12,512]{1,0:T(8,128)} %get-tuple-element.407, pred[512,1024]{1,0:T(8,128)(4,1)} %broadcast_compare_fusion.9), kind=kLoop, calls=%fused_computation.108 | loop fusion | flops 37748736 | bytes 63488000 | tf_op jit(solution)/shard_map/while/body/eval_jaxpr/cond/branch_0_fun/convert_element_type | solution.py:130
  355.6 10.2 convolution_multiply_fusion.4
  368.8 8.8 convolution_multiply_fusion.3
  381.1 13.4 %fusion.58 = f32[12,1024,64]{1,2,0:T(8,128)} fusion(bf16[512,12,64]{0,2,1:T(8,128)(2,1)} %bitcast.315, f32[12,512,1024]{2,1,0:T(8,128)} %fusion.177, f32[12,512]{1,0:T(8,128)} %get-tuple-element.407, pred[512,1024]{1,0:T(8,128)(4,1)} %broadcast_compare_fusion.9), kind=kOutput, calls=%fused_computation.112 | convolution fusion | flops 830472192 | bytes 29646848 | tf_op jit(solution)/shard_map/while/body/eval_jaxpr/cond/branch_0_fun/hqk,qhd->khd/dot_general | solution.py:138
  394.5 3.6 copy.377
  418.8 87.9 %conditional.6 = (f32[512,768]{1,0:T(8,128)}, f32[1024,768]{1,0:T(8,128)}, f32[1024,768]{1,0:T(8,128)}, f32[512,768]{0,1:T(8,128)}, f32[1024,768]{1,0:T(8,128)}, /*index=5*/f32[1024,768]{1,0:T(8,128)}) conditional(s32[]{:T(128)} %convert_element_type.235, (s32[512]{0:T(512)S(1)}, s32[1024]{0:T(1024)S(1)}, bf16[512,768]{1,0:T(8,128)(2,1)}, ...), branch_computations={%region_22.24_spmd, %region_24.27_spmd} | conditional | flops 2126094336 | bytes 243964368 | solution.py:294
  425.8 7.8 fusion.176
  440.7 11.4 multiply_reduce_fusion
  453.6 7.1 multiply_convert_fusion
  466.8 6.2 convolution_multiply_fusion.1
  479.3 7.4 fusion.35
  506.7 4.3 fusion.129
  512.3 4.4 fusion.130
  521.1 12.4 maximum_multiply_fusion.1
  535.9 3.5 copy.441
  539.5 3.5 copy.432
  543.0 13.7 %fusion.121 = bf16[1024,768]{1,0:T(8,128)(2,1)} fusion(f32[1024,768]{1,0:T(8,128)} %copy.441, f32[512,768]{1,0:T(8,128)} %get-tuple-element.452, f32[512,768]{1,0:T(8,128)} %get-tuple-element.450, f32[768]{0:T(1024)S(1)} %copy-done.66), kind=kLoop, calls=%fused_computation.206 | loop fusion | flops 3932160 | bytes 7867392 | tf_op jit(solution)/shard_map/convert
  556.7 255.6 %collective-permute-done.2 = bf16[1,1024,768]{2,1,0:T(8,128)(2,1)} collective-permute-done((bf16[1,1024,768]{2,1,0:T(8,128)(2,1)}, bf16[1,1024,768]{2,1,0:T(8,128)(2,1)}, u32[]{:S(2)}, u32[]{:S(2)}) %collective-permute-start.2) | collective-permute-done | bytes 1572896 | tf_op jit(solution)/shard_map/ppermute | solution.py:21
  812.3 15.8 %fusion.119 = (f32[1,1024,768]{2,1,0:T(8,128)}, f32[1,1024,768]{2,1,0:T(8,128)}) fusion(f32[1,1024,768]{2,1,0:T(8,128)S(1)} %copy-done.26, f32[1,512,768]{2,1,0:T(8,128)} %bitcast.84, f32[1,512,768]{2,1,0:T(8,128)} %bitcast.83, f32[768]{0:T(1024)S(1)} %copy-done.66, bf16[1,1024,768]{2,1,0:T(8,128)(2,1)} %collective-permute-done.2, ...), kind=kLoop, calls=%fused_computation.200 | loop fusion | flops 6291456 | bytes 20450304 | tf_op jit(solution)/shard_map/add | solution.py:404
  828.2 3.6 copy.435
  835.8 3.5 copy.436
  839.3 4.9 collective-permute-done.3
  844.2 5.7 convert_bitcast_fusion.1
  850.0 13.3 %convert_bitcast_fusion.2 = (bf16[1024,768]{1,0:T(8,128)(2,1)S(1)}, f32[1,1024,768]{2,1,0:T(8,128)}) fusion(f32[1,1024,768]{2,1,0:T(8,128)S(1)} %copy-done.23, f32[768]{0:T(1024)S(1)} %copy-done.66, bf16[1,1024,768]{2,1,0:T(8,128)(2,1)} %collective-permute-done.2, f32[1024,768]{1,0:T(8,128)} %get-tuple-element.453, f32[1024,768]{1,0:T(8,128)} %get-tuple-element.454), kind=kLoop, calls=%fused_computation.242 | loop fusion | flops 5505024 | bytes 15731712 | tf_op jit(solution)/shard_map/concatenate | solution.py:406
  863.3 7.1 fusion.91
  871.1 10.6 fusion.122
  882.4 13.9 %fusion.134 = f32[3072,768]{1,0:T(8,128)} fusion(bf16[1,1,1024,768]{3,2,1,0:T(8,128)(2,1)} %param.48, f32[1024,3072]{1,0:T(8,128)} %copy-done.20, f32[3072]{0:T(1024)S(1)} %copy-done.88), kind=kOutput, calls=%fused_computation.238 | convolution fusion | flops 4863295488 | bytes 23605248 | tf_op jit(solution)/shard_map/dot_general | solution.py:310
  899.6 12.3 fusion.145
  914.4 9.9 fusion.173
  924.3 3.6 copy.439
  927.9 4.7 fusion.86
  935.1 62.0 %all-reduce.17 = (bf16[768]{0:T(1024)(128)(2,1)}, bf16[768]{0:T(1024)(128)(2,1)}, bf16[2304]{0:T(1024)(128)(2,1)}, bf16[768]{0:T(1024)(128)(2,1)}, bf16[768]{0:T...) all-reduce(f32[768]{0:T(1024)} %get-tuple-element.798, ...), channel_id=2, replica_groups=mesh['stream'=2,'batch'=16] {'batch'}, use_global_device_ids=true, to_apply=%region_35.36.clone | all-reduce | flops 9984 | bytes 59904
  1007.2 11.2 all-reduce.18
  1031.1 50.7 %reduce-scatter.9.cloned.1.call-done = f32[48,3072]{1,0:T(8,128)} async-done(((f32[768,3072]{1,0:T(8,128)}), f32[48,3072]{1,0:T(8,128)}) %reduce-scatter.9.cloned.1.call-update) | async-done | bytes 589840 | tf_op jit(solution)/shard_map/reduce_scatter | solution.py:427
  1083.6 113.8 %reduce-scatter.11.cloned.1.call-done = f32[192,768]{1,0:T(8,128)} async-done(((f32[3072,768]{1,0:T(8,128)}), f32[192,768]{1,0:T(8,128)}) %reduce-scatter.11.cloned.1.call-update) | async-done | bytes 589840 | tf_op jit(solution)/shard_map/reduce_scatter | solution.py:429
  1200.0 6.0 fusion.111
  1205.9 3.6 copy.444
  1209.5 28.2 %all-reduce.22.cloned.1.call-done = (bf16[48,2304]{1,0:T(8,128)(2,1)}, bf16[48,768]{1,0:T(8,128)(2,1)}, bf16[48,3072]{1,0:T(8,128)(2,1)}, bf16[192,768]{1,0:T(8,128)(2,1)}) async-done(((bf16[48,2304]{1,0:T(8,128)(2,1)}, bf16[48,768]{1,0:T(8,128)(2,1)}, bf16[48,3072]{1,0:T(8,128)(2,1)}, bf16[192,768]{1,0:T(8,128)(2,1)}), (bf16[48,2304]{1,0:T(8,128)(2,1)}, bf16[48,768]{1,0:T(8,128)(2,1)}, ...) | async-done | bytes 884752 | tf_op jit(solution)/shard_map/psum | solution.py:448
  (252 shorter events, 189.2 us)
Async XLA Ops:
  7.2 7.1 copy-start
  7.2 1020.6 %reduce-scatter.7.cloned.1.call-start = ((), (), s32[]{:S(2)}) async-start(), calls=%async_computation.5 | async-start | bytes 2506752 | tf_op jit(solution)/shard_map/reduce_scatter | solution.py:423
  7.3 39.2 %copy-start.65 = (f32[768]{0:T(1024)}, f32[768]{0:T(1024)S(1)}, u32[]{:S(2)}) copy-start(f32[768]{0:T(1024)S(1)} %fusion.156) | copy-start | bytes 9220
  7.3 7.1 copy-start.80
  7.3 7.1 copy-start.90
  10.0 4.3 copy-start.6
  10.0 4.3 copy-start.86
  11.8 1.9 copy-start.72
  18.6 5.5 copy-start.11
  61.2 40.0 %collective-permute-start = (bf16[1,1024,768]{2,1,0:T(8,128)(2,1)}, bf16[1,1024,768]{2,1,0:T(8,128)(2,1)}, u32[]{:S(2)}, u32[]{:S(2)}) collective-permute-start(bf16[1,1024,768]{2,1,0:T(8,128)(2,1)} %get-tuple-element.856), channel_id=1, source_target_pairs={{0,16},{1,17},{2,18},{3,19},{4,20},{5,21},{6,22},{7,23},{8,24},{9,... | collective-permute-start | bytes 4718600 | tf_op jit(solution)/shard_map/ppermute | solution.py:21
  70.5 63.3 %collective-permute-start.1 = (bf16[1,1024,768]{2,1,0:T(8,128)(2,1)}, bf16[1,1024,768]{2,1,0:T(8,128)(2,1)}, u32[]{:S(2)}, u32[]{:S(2)}) collective-permute-start(bf16[1,1024,768]{2,1,0:T(8,128)(2,1)} %slice.336), channel_id=1, source_target_pairs={{0,16},{1,17},{2,18},{3,19},{4,20},{5,21},{6,22},{7,23},{8,24},{9,... | collective-permute-start | bytes 4718600 | tf_op jit(solution)/shard_map/ppermute | solution.py:21
  76.3 57.4 %copy-start.67 = (s32[512]{0:T(512)}, s32[512]{0:T(512)S(1)}, u32[]{:S(2)}) copy-start(s32[512]{0:T(512)S(1)} %get-tuple-element.876) | copy-start | bytes 6148
  76.3 99.0 %copy-start.70 = (s32[512]{0:T(512)}, s32[512]{0:T(512)S(1)}, u32[]{:S(2)}) copy-start(s32[512]{0:T(512)S(1)} %get-tuple-element.875) | copy-start | bytes 6148
  145.3 4.6 copy-start.3
  175.3 58.3 %copy-start.89 = (f32[768]{0:T(1024)S(1)}, f32[768]{0:T(1024)}, u32[]{:S(2)}) copy-start(f32[768]{0:T(1024)} %param.55) | copy-start | bytes 9220
  181.3 14.4 %copy-start.33 = (pred[512,1024]{1,0:T(8,128)(4,1)S(1)}, pred[512,1024]{1,0:T(8,128)(4,1)}, u32[]{:S(2)}) copy-start(pred[512,1024]{1,0:T(8,128)(4,1)} %broadcast_compare_fusion.3) | copy-start | bytes 1572868 | tf_op jit(solution)/shard_map/while/body/eval_jaxpr/cond
  231.3 7.9 slice-start.3
  233.6 5.6 slice-start.4
  237.6 44.3 %copy-start.52 = (f32[1024]{0:T(1024)}, f32[1024]{0:T(1024)S(1)}, u32[]{:S(2)}) copy-start(f32[1024]{0:T(1024)S(1)} %broadcast_multiply_fusion.4) | copy-start | bytes 12292
  239.2 42.6 %copy-start.56 = (f32[1024]{0:T(1024)}, f32[1024]{0:T(1024)S(1)}, u32[]{:S(2)}) copy-start(f32[1024]{0:T(1024)S(1)} %add_rsqrt_fusion) | copy-start | bytes 12292
  239.2 5.6 copy-start.43
  239.2 5.6 copy-start.87
  244.8 18.3 %copy-start.20 = (f32[1024,3072]{1,0:T(8,128)}, f32[1024,3072]{1,0:T(8,128)S(1)}, u32[]{:S(2)}) copy-start(f32[1024,3072]{1,0:T(8,128)S(1)} %fusion.163) | copy-start | bytes 37748740
  277.2 4.6 copy-start.5
  277.3 4.7 copy-start.10
  281.9 3.9 copy-start.85
  285.8 1.7 copy-start.24
  440.7 11.5 slice-start
  440.7 11.5 slice-start.1
  440.7 12.9 %slice-start.2 = ((s8[12582912]{0:T(1024)(128)(4,1)}), s8[4194304]{0:T(1024)(128)(4,1)S(1)}, s32[]{:S(2)}) async-start(s8[12582912]{0:T(1024)(128)(4,1)} %bitcast.260), calls=%async_computation.11 | async-start | bytes 8388608 | tf_op jit(solution)/shard_map/while/body/eval_jaxpr/cond
  440.7 12.9 %copy-start.38 = (pred[512,512]{0,1:T(8,128)(4,1)S(1)}, pred[512,512]{0,1:T(8,128)(4,1)}, u32[]{:S(2)}) copy-start(pred[512,512]{0,1:T(8,128)(4,1)} %broadcast_compare_fusion.6) | copy-start | bytes 786436 | tf_op jit(solution)/shard_map/while/body/eval_jaxpr/cond
  440.7 12.9 %copy-start.45 = (f32[12,512]{1,0:T(8,128)S(1)}, f32[12,512]{1,0:T(8,128)}, u32[]{:S(2)}) copy-start(f32[12,512]{1,0:T(8,128)} %get-tuple-element.391) | copy-start | bytes 73732 | tf_op jit(solution)/shard_map/while/body/eval_jaxpr/cond
  453.6 7.1 copy-start.29
  460.7 3.0 copy-start.2
  475.9 3.4 copy-start.35
  475.9 3.4 copy-start.39
  475.9 3.4 copy-start.46
  511.0 301.3 %collective-permute-start.2 = (bf16[1,1024,768]{2,1,0:T(8,128)(2,1)}, bf16[1,1024,768]{2,1,0:T(8,128)(2,1)}, u32[]{:S(2)}, u32[]{:S(2)}) collective-permute-start(bf16[1,1024,768]{2,1,0:T(8,128)(2,1)} %fusion.129), channel_id=1, source_target_pairs={{16,0},{17,1},{18,2},{19,3},{20,4},{21,5},{22,6},{23,7},{24,8},{25... | collective-permute-start | bytes 4718600 | tf_op jit(solution)/shard_map/ppermute | solution.py:21
  512.3 5.9 copy-start.25
  512.3 5.9 copy-start.60
  516.7 4.4 copy-start.75
  516.7 327.5 %collective-permute-start.3 = (bf16[1,1024,768]{2,1,0:T(8,128)(2,1)}, bf16[1,1024,768]{2,1,0:T(8,128)(2,1)}, u32[]{:S(2)}, u32[]{:S(2)}) collective-permute-start(bf16[1,1024,768]{2,1,0:T(8,128)(2,1)} %fusion.130), channel_id=1, source_target_pairs={{16,0},{17,1},{18,2},{19,3},{20,4},{21,5},{22,6},{23,7},{24,8},{25... | collective-permute-start | bytes 4718600 | tf_op jit(solution)/shard_map/ppermute | solution.py:21
  521.1 508.3 %reduce-scatter.5.cloned.1.call-start = ((), (), s32[]{:S(2)}) async-start(), calls=%async_computation.4 | async-start | bytes 7520256 | tf_op jit(solution)/shard_map/reduce_scatter | solution.py:421
  539.5 3.5 copy-start.66
  543.0 269.3 %copy-start.26 = (f32[1,1024,768]{2,1,0:T(8,128)S(1)}, f32[1,1024,768]{2,1,0:T(8,128)}, u32[]{:S(2)}) copy-start(f32[1,1024,768]{2,1,0:T(8,128)} %copy.432) | copy-start | bytes 9437188
  844.2 5.7 copy-start.23
  849.9 13.3 %copy-start.7 = (bf16[1,1,1024,768]{2,3,1,0:T(8,128)(2,1)S(1)}, bf16[1,1,1024,768]{2,3,1,0:T(8,128)(2,1)}, u32[]{:S(2)}) copy-start(bf16[1,1,1024,768]{2,3,1,0:T(8,128)(2,1)} %copy.394) | copy-start | bytes 4718596
  849.9 13.3 %copy-start.42 = (bf16[1024,768]{1,0:T(8,128)(2,1)S(1)}, bf16[1024,768]{1,0:T(8,128)(2,1)}, u32[]{:S(2)}) copy-start(bf16[1024,768]{1,0:T(8,128)(2,1)} %fusion.121) | copy-start | bytes 4718596
  849.9 13.3 %copy-start.73 = (f32[1024]{0:T(1024)S(1)}, f32[1024]{0:T(1024)}, u32[]{:S(2)}) copy-start(f32[1024]{0:T(1024)} %copy-done.72) | copy-start | bytes 12292
  849.9 13.3 %copy-start.77 = (f32[1024]{0:T(1024)S(1)}, f32[1024]{0:T(1024)}, u32[]{:S(2)}) copy-start(f32[1024]{0:T(1024)} %copy-done.76) | copy-start | bytes 12292
  849.9 13.3 %copy-start.81 = (f32[768]{0:T(1024)S(1)}, f32[768]{0:T(1024)}, u32[]{:S(2)}) copy-start(f32[768]{0:T(1024)} %param.50) | copy-start | bytes 9220
  850.0 13.3 %copy-start.91 = (f32[768]{0:T(1024)S(1)}, f32[768]{0:T(1024)}, u32[]{:S(2)}) copy-start(f32[768]{0:T(1024)} %param.51) | copy-start | bytes 9220
  870.4 211.4 %reduce-scatter.9.cloned.1.call-start = ((), (), s32[]{:S(2)}) async-start(), calls=%async_computation.6 | async-start | bytes 10027008 | tf_op jit(solution)/shard_map/reduce_scatter | solution.py:427
  881.7 315.7 %reduce-scatter.11.cloned.1.call-start = ((), (), s32[]{:S(2)}) async-start(), calls=%async_computation.7 | async-start | bytes 10027008 | tf_op jit(solution)/shard_map/reduce_scatter | solution.py:429
  896.3 3.3 copy-start.92
  896.3 341.4 %all-reduce.22.cloned.1.call-start = ((), (), s32[]{:S(2)}) async-start(), calls=%async_computation.8 | async-start | bytes 1769472 | tf_op jit(solution)/shard_map/psum | solution.py:448
  927.9 4.7 copy-start.8
  927.9 5.5 copy-start.9
  927.9 5.5 copy-start.74
  927.9 5.5 copy-start.78
  927.9 5.5 copy-start.82
  997.1 202.8 %copy-start.84 = (f32[1024]{0:T(1024)S(1)}, f32[1024]{0:T(1024)}, u32[]{:S(2)}) copy-start(f32[1024]{0:T(1024)} %get-tuple-element.800) | copy-start | bytes 12292
  997.1 202.8 %copy-start.79 = (f32[1024]{0:T(1024)S(1)}, f32[1024]{0:T(1024)}, u32[]{:S(2)}) copy-start(f32[1024]{0:T(1024)} %copy-done.76) | copy-start | bytes 12292
  997.1 202.8 %copy-start.83 = (f32[768]{0:T(1024)S(1)}, f32[768]{0:T(1024)}, u32[]{:S(2)}) copy-start(f32[768]{0:T(1024)} %param.50) | copy-start | bytes 9220
  (11 other events, 11.0 us)
Sparse Core Ops, SparseCore 0:
  521.2 329.4 reduce-scatter.6
  870.5 96.1 reduce-scatter.4
  970.8 110.9 reduce-scatter.8
  1086.3 111.0 reduce-scatter.10
  1200.9 36.7 all-reduce.21
where the time goes:
time: 1260 us; the launch traced here: 1250 us
  waiting for transfers between devices  504 us (40%)
  matrix products  240 us (19%)
  other arithmetic  199 us (16%)
  local copies, waits for them, and re-layouts  165 us (13%)
  blocking collectives  73.2 us (6%)
  loops' own time  40.9 us (3%)
  between operations  17.2 us (1%)
    ppermute x4, waiting for transfers between devices, shifted(): return lax.ppermute(block, axis, route)  311 us
    reduce_scatter x1, waiting for transfers between devices, local(): lax.psum_scatter(downw_grad, 'batch', scatter_dimension=0, tiled=True)  114 us
    unnamed x1, blocking collectives  62 us
    another operation x21, local copies, waits for them, and re-layouts  51.7 us
    reduce_scatter x1, waiting for transfers between devices, local(): lax.psum_scatter(upw_grad, 'batch', scatter_dimension=0, tiled=True)  50.7 us
    dot_general x4, matrix products, times_transpose(): lax.dot_general(left, right, (((1,), (1,)), ((), ())), preferred_element_...  40 us
    dot_general x4, matrix products, scores_of(): jnp.einsum('qhd,khd->hqk', head_view(query), head_view(keys), preferred_e...  39.1 us
    dot_general x4, matrix products, outer(): lax.dot_general(left, right, (((0,), (0,)), ((), ())), preferred_element_...  34.5 us
  transfers between devices with their start and end apart: 9, of which 7 were waited for; matrix products, arithmetic and copies ran while one was open for 16% of the time, Pallas kernels for 0%

commit v1 on v0

v1 whole, which is shorter than its diff:
```python
from functools import partial
import math

import jax
import jax.numpy as jnp
from jax import lax
from jax.experimental import pallas as pl
from jax.experimental.pallas import tpu as pltpu
from jax.sharding import PartitionSpec as P
import numpy as np

HEAD = 64
PAIR = 2 * HEAD
ROWS = 256
TILE = 256

masked_value = -1e30
epsilon = 1e-05
low = jnp.bfloat16
wide = jnp.float32
score_scale = math.log2(math.e) / math.sqrt(HEAD)
ln2 = math.log(2.0)
gelu_c = math.sqrt(2.0 / math.pi)
gelu_k = 0.044715
mega = 1024 * 1024


def dot_nn(left, right):
    return lax.dot_general(left, right, (((1,), (0,)), ((), ())), preferred_element_type=wide)


def dot_nt(left, right):
    return lax.dot_general(left, right, (((1,), (1,)), ((), ())), preferred_element_type=wide)


def dot_tn(left, right):
    return lax.dot_general(left, right, (((0,), (0,)), ((), ())), preferred_element_type=wide)


def params(limit_mib):
    return pltpu.CompilerParams(
        dimension_semantics=("arbitrary",), vmem_limit_bytes=limit_mib * mega
    )


def cost(flops, nbytes, trans=0):
    return pl.CostEstimate(
        flops=int(flops), bytes_accessed=int(nbytes), transcendentals=int(trans)
    )


def whole_spec(shape):
    zeros = (0,) * len(shape)
    return pl.BlockSpec(shape, lambda *_: zeros, pipeline_mode=pl.Buffered(1))


def row_spec(width, rows=ROWS):
    return pl.BlockSpec((rows, width), lambda i: (i, 0))


def normalize(values):
    mean = jnp.mean(values, axis=-1, keepdims=True)
    centred = values - mean
    factor = lax.rsqrt(jnp.mean(centred * centred, axis=-1, keepdims=True) + epsilon)
    return (centred * factor, factor)


def norm_back(grad_normed, normed, factor):
    first = jnp.mean(grad_normed, axis=-1, keepdims=True)
    second = jnp.mean(grad_normed * normed, axis=-1, keepdims=True)
    return factor * (grad_normed - first - normed * second)


def rotary_tables(length):
    places = np.arange(length, dtype=np.float64)[:, None]
    column = np.arange(PAIR) % HEAD
    angle = places * (10000.0 ** (-2.0 * (column % (HEAD // 2)) / HEAD))[None, :]
    upper = (column >= HEAD // 2)[None, :]
    cosine, sine = np.cos(angle), np.sin(angle)
    tables = (cosine, np.where(upper, sine, 0.0), np.where(upper, 0.0, -sine))
    return tuple(jnp.asarray(t, dtype=wide) for t in tables)


def rotate(values, cosine, sine_a, sine_b):
    return (
        values * cosine
        + pltpu.roll(values, HEAD // 2, 1) * sine_a
        + pltpu.roll(values, PAIR - HEAD // 2, 1) * sine_b
    )


def rotate_back(values, cosine, sine_a, sine_b):
    return (
        values * cosine
        - pltpu.roll(values, HEAD // 2, 1) * sine_a
        - pltpu.roll(values, PAIR - HEAD // 2, 1) * sine_b
    )


def project_kernel(x_ref, w_ref, bias_ref, gain1_ref, bias1_ref, cos_ref, sa_ref, sb_ref,
                   h_ref, q_ref, k_ref, v_ref):
    width = x_ref.shape[1]
    normed, _ = normalize(x_ref[...].astype(wide))
    hidden = (normed * gain1_ref[...] + bias1_ref[...]).astype(low)
    h_ref[...] = hidden
    cosine, sa, sb = cos_ref[...], sa_ref[...], sb_ref[...]
    for out, part in ((q_ref, 0), (k_ref, 1), (v_ref, 2)):
        cols = slice(part * width, (part + 1) * width)
        mixed = dot_nn(hidden, w_ref[:, cols]) + bias_ref[:, cols]
        if part == 2:
            out[...] = mixed.astype(low)
            continue
        for group in range(width // PAIR):
            at = slice(group * PAIR, (group + 1) * PAIR)
            turned = rotate(mixed[:, at], cosine, sa, sb)
            if part == 0:
                turned = turned * score_scale
            out[:, at] = turned.astype(low)


def project_far_kernel(noisy_ref, x_ref, far_ref, wk_ref, wv_ref, bias_ref, gain1_ref, bias1_ref,
                       cos_ref, sa_ref, sb_ref, h_ref, k_ref, v_ref):
    width = x_ref.shape[1]
    source = jnp.where(noisy_ref[0] == 1, far_ref[...].astype(wide), x_ref[...].astype(wide))
    normed, _ = normalize(source)
    hidden = (normed * gain1_ref[...] + bias1_ref[...]).astype(low)
    h_ref[...] = hidden
    cosine, sa, sb = cos_ref[...], sa_ref[...], sb_ref[...]
    mixed = dot_nn(hidden, wk_ref[...]) + bias_ref[:, width : 2 * width]
    for group in range(width // PAIR):
        at = slice(group * PAIR, (group + 1) * PAIR)
        k_ref[:, at] = rotate(mixed[:, at], cosine, sa, sb).astype(low)
    mixed = dot_nn(hidden, wv_ref[...]) + bias_ref[:, 2 * width :]
    v_ref[...] = mixed.astype(low)


def project(x, weight, bias, gain1, bias1, tables):
    count, width = x.shape
    row = jax.ShapeDtypeStruct((count, width), low)
    return pl.pallas_call(
        project_kernel,
        grid=(count // ROWS,),
        in_specs=[
            row_spec(width),
            whole_spec(weight.shape),
            whole_spec(bias.shape),
            whole_spec(gain1.shape),
            whole_spec(bias1.shape),
            row_spec(PAIR),
            row_spec(PAIR),
            row_spec(PAIR),
        ],
        out_specs=[row_spec(width)] * 4,
        out_shape=[row] * 4,
        compiler_params=params(40),
        cost_estimate=cost(2 * count * width * 3 * width, 16e6),
        name="project",
    )(x, weight, bias, gain1, bias1, *tables)


def project_far(noisy, x, far, weight, bias, gain1, bias1, tables):
    count, width = x.shape
    row = jax.ShapeDtypeStruct((count, width), low)
    return pl.pallas_call(
        project_far_kernel,
        grid=(count // ROWS,),
        in_specs=[
            pl.BlockSpec(memory_space=pltpu.SMEM),
            row_spec(width),
            row_spec(width),
            pl.BlockSpec((width, width), lambda i: (0, 1), pipeline_mode=pl.Buffered(1)),
            pl.BlockSpec((width, width), lambda i: (0, 2), pipeline_mode=pl.Buffered(1)),
            whole_spec(bias.shape),
            whole_spec(gain1.shape),
            whole_spec(bias1.shape),
            row_spec(PAIR),
            row_spec(PAIR),
            row_spec(PAIR),
        ],
        out_specs=[row_spec(width)] * 3,
        out_shape=[row] * 3,
        compiler_params=params(40),
        cost_estimate=cost(2 * count * width * 2 * width, 12e6),
        name="project_far",
    )(noisy, x, far, weight, weight, bias, gain1, bias1, *tables)


def head_masks():
    lane = lax.broadcasted_iota(jnp.int32, (1, PAIR), 1)
    return (lane < HEAD, lane >= HEAD)


def attend_kernel(krow_ref, qcol_ref, q_ref, kn_ref, vn_ref, kf_ref, vf_ref, o_ref, lse_ref):
    length = q_ref.shape[0]
    kb, qb = krow_ref[...], qcol_ref[...]
    near = kb == qb
    far = kb < qb
    masks = head_masks()
    vf_t = vf_ref[...].astype(wide).T.astype(low)
    vn_t = vn_ref[...].astype(wide).T.astype(low)
    for tile in range(length // TILE):
        here = slice(tile * TILE, (tile + 1) * TILE)
        query = q_ref[here, :]
        pieces = []
        for head in range(2):
            rows = slice(head * HEAD, (head + 1) * HEAD)
            mine = jnp.where(masks[head], query, jnp.zeros_like(query))
            scores_near = dot_nt(kn_ref[here, :], mine)
            scores_diag = dot_nt(kf_ref[here, :], mine)
            diag = jnp.where(near, scores_near, jnp.where(far, scores_diag, masked_value))
            top = jnp.max(diag, axis=0, keepdims=True)
            if tile:
                past = dot_nt(kf_ref[: tile * TILE, :], mine)
                top = jnp.maximum(top, jnp.max(past, axis=0, keepdims=True))
            prob = jnp.exp2(diag - top)
            total = jnp.sum(prob, axis=0, keepdims=True)
            prob_near = jnp.where(near, prob, 0.0).astype(low)
            prob_far = jnp.where(near, 0.0, prob).astype(low)
            mixed = dot_nn(vn_t[rows, here], prob_near) + dot_nn(vf_t[rows, here], prob_far)
            if tile:
                prob = jnp.exp2(past - top)
                total = total + jnp.sum(prob, axis=0, keepdims=True)
                mixed = mixed + dot_nn(vf_t[rows, : tile * TILE], prob.astype(low))
            lse_ref[0, head : head + 1, here] = top + jnp.log2(total)
            pieces.append(mixed * (1.0 / total))
        o_ref[here, :] = jnp.concatenate(pieces, axis=0).T.astype(low)


def attend(krow, qcol, q, kn, vn, kf, vf):
    count, width = q.shape
    pairs = width // PAIR
    pair_spec = pl.BlockSpec((count, PAIR), lambda p: (0, p))
    return pl.pallas_call(
        attend_kernel,
        grid=(pairs,),
        in_specs=[whole_spec(krow.shape), whole_spec(qcol.shape)] + [pair_spec] * 5,
        out_specs=[pair_spec, pl.BlockSpec((1, 2, count), lambda p: (p, 0, 0))],
        out_shape=[
            jax.ShapeDtypeStruct((count, width), low),
            jax.ShapeDtypeStruct((pairs, 2, count), wide),
        ],
        compiler_params=params(48),
        cost_estimate=cost(20e9, 10e6, 6e6),
        name="attend",
    )(krow, qcol, q, kn, vn, kf, vf)


def middle_kernel(x_ref, o_ref, g_ref, wp_ref, bp_ref, gain2_ref, bias2_ref, wu_ref, bu_ref,
                  wd_ref, bd_ref, out_ref, h2_ref, a_ref, du_ref, dy_ref, dyl_ref, do_ref,
                  downb_ref, upb_ref, gain2g_ref, bias2g_ref, projb_ref):
    width = x_ref.shape[1]
    ff = wu_ref.shape[1]

    @pl.when(pl.program_id(0) == 0)
    def _():
        for ref in (downb_ref, upb_ref, gain2g_ref, bias2g_ref, projb_ref):
            ref[...] = jnp.zeros_like(ref)

    y = x_ref[...].astype(wide) + dot_nn(o_ref[...], wp_ref[...]) + bp_ref[...]
    normed, factor = normalize(y)
    hidden = (normed * gain2_ref[...] + bias2_ref[...]).astype(low)
    h2_ref[...] = hidden
    grad = g_ref[...]
    grad_wide = grad.astype(wide)
    result = y + bd_ref[...]
    dh2 = jnp.zeros_like(y)
    for part in range(ff // width):
        cols = slice(part * width, (part + 1) * width)
        up = dot_nn(hidden, wu_ref[:, cols]) + bu_ref[:, cols]
        da = dot_nt(grad, wd_ref[cols, :])
        square = up * up
        half = 0.5 + 0.5 * jnp.tanh(up * (gelu_c + (gelu_c * gelu_k) * square))
        active = (up * half).astype(low)
        slope = half + (up * (2.0 * gelu_c + (6.0 * gelu_c * gelu_k) * square)) * (
            half * (1.0 - half)
        )
        du = da * slope
        du_low = du.astype(low)
        a_ref[:, cols] = active
        du_ref[:, cols] = du_low
        upb_ref[:, cols] += jnp.sum(du, axis=0, keepdims=True)
        result = result + dot_nn(active, wd_ref[cols, :])
        dh2 = dh2 + dot_nt(du_low, wu_ref[:, cols])
    out_ref[...] = result.astype(low)
    downb_ref[...] += jnp.sum(grad_wide, axis=0, keepdims=True)
    gain2g_ref[...] += jnp.sum(dh2 * normed, axis=0, keepdims=True)
    bias2g_ref[...] += jnp.sum(dh2, axis=0, keepdims=True)
    dy = grad_wide + norm_back(dh2 * gain2_ref[...], normed, factor)
    dy_ref[...] = dy
    projb_ref[...] += jnp.sum(dy, axis=0, keepdims=True)
    dy_low = dy.astype(low)
    dyl_ref[...] = dy_low
    do_ref[...] = dot_nt(dy_low, wp_ref[...]).astype(low)


def middle(x, o, g, wp, bp, gain2, bias2, wu, bu, wd, bd):
    count, width = x.shape
    ff = wu.shape[1]
    row = jax.ShapeDtypeStruct((count, width), low)
    vec = jax.ShapeDtypeStruct((1, width), wide)
    return pl.pallas_call(
        middle_kernel,
        grid=(count // ROWS,),
        in_specs=[row_spec(width)] * 3
        + [whole_spec(a.shape) for a in (wp, bp, gain2, bias2, wu, bu, wd, bd)],
        out_specs=[
            row_spec(width),
            row_spec(width),
            row_spec(ff),
            row_spec(ff),
            row_spec(width),
            row_spec(width),
            row_spec(width),
        ]
        + [whole_spec((1, n)) for n in (width, ff, width, width, width)],
        out_shape=[
            row,
            row,
            jax.ShapeDtypeStruct((count, ff), low),
            jax.ShapeDtypeStruct((count, ff), low),
            jax.ShapeDtypeStruct((count, width), wide),
            row,
            row,
            vec,
            jax.ShapeDtypeStruct((1, ff), wide),
            vec,
            vec,
            vec,
        ],
        compiler_params=params(52),
        cost_estimate=cost(2 * count * width * (4 * ff + 2 * width), 40e6, count * ff),
        name="middle",
    )(x, o, g, wp, bp, gain2, bias2, wu, bu, wd, bd)


def outer_kernel(left_ref, right_ref, out_ref):
    out_ref[...] = dot_tn(left_ref[...], right_ref[...]).astype(low)


def outer(left, right, tile=256):
    count, tall = left.shape
    width = right.shape[1]
    return pl.pallas_call(
        outer_kernel,
        grid=(tall // tile,),
        in_specs=[pl.BlockSpec((count, tile), lambda i: (0, i)), whole_spec(right.shape)],
        out_specs=pl.BlockSpec((tile, width), lambda i: (i, 0)),
        out_shape=jax.ShapeDtypeStruct((tall, width), low),
        compiler_params=params(48),
        cost_estimate=cost(2 * count * tall * width, 2 * (tall * width + count * (tall + width))),
        name="outer",
    )(left, right)


def attend_back_kernel(krow_ref, qcol_ref, q_ref, kn_ref, vn_ref, kf_ref, vf_ref, do_ref, o_ref,
                       lse_ref, cos_ref, sa_ref, sb_ref,
                       dq_ref, dkn_ref, dvn_ref, dkf_ref, dvf_ref, sums_ref,
                       dqt_acc, dkf_acc, dvf_acc):
    length = q_ref.shape[0]
    kb, qb = krow_ref[...], qcol_ref[...]
    near = kb == qb
    far = kb < qb
    masks = head_masks()
    kf_t = kf_ref[...].astype(wide).T.astype(low)
    kn_t = kn_ref[...].astype(wide).T.astype(low)
    product = do_ref[...].astype(wide) * o_ref[...].astype(wide)
    high = product.astype(low)
    rest = (product - high.astype(wide)).astype(low)
    head_row = lax.broadcasted_iota(jnp.int32, (8, PAIR), 0)
    head_lane = lax.broadcasted_iota(jnp.int32, (8, PAIR), 1) // HEAD
    picker = jnp.where(head_row == head_lane, 1.0, 0.0).astype(low)
    deltas = dot_nt(picker, high) + dot_nt(picker, rest)
    cosine, sa, sb = cos_ref[...], sa_ref[...], sb_ref[...]
    sum_q = jnp.zeros((1, PAIR), wide)
    sum_kn = jnp.zeros((1, PAIR), wide)
    sum_vn = jnp.zeros((1, PAIR), wide)
    for tile in range(length // TILE):
        here = slice(tile * TILE, (tile + 1) * TILE)
        query, grad = q_ref[here, :], do_ref[here, :]
        dkn = jnp.zeros((TILE, PAIR), wide)
        dvn = jnp.zeros((TILE, PAIR), wide)
        for head in range(2):
            rows = slice(head * HEAD, (head + 1) * HEAD)
            mine = jnp.where(masks[head], query, jnp.zeros_like(query))
            grad_mine = jnp.where(masks[head], grad, jnp.zeros_like(grad))
            lse = lse_ref[0, head : head + 1, here]
            delta = deltas[head : head + 1, here]
            scores = jnp.where(
                near,
                dot_nt(kn_ref[here, :], mine),
                jnp.where(far, dot_nt(kf_ref[here, :], mine), masked_value),
            )
            prob = jnp.exp2(scores - lse)
            dprob = jnp.where(
                near, dot_nt(vn_ref[here, :], grad_mine), dot_nt(vf_ref[here, :], grad_mine)
            )
            dscore = prob * (dprob - delta)
            prob_near = jnp.where(near, prob, 0.0).astype(low)
            prob_far = jnp.where(near, 0.0, prob).astype(low)
            ds_near = jnp.where(near, dscore, 0.0).astype(low)
            ds_far = jnp.where(near, 0.0, dscore).astype(low)
            dkn = dkn + dot_nn(ds_near, mine)
            dvn = dvn + dot_nn(prob_near, grad_mine)
            dkf = dot_nn(ds_far, mine)
            dvf = dot_nn(prob_far, grad_mine)
            if head:
                dkf_acc[here, :] += dkf
                dvf_acc[here, :] += dvf
            else:
                dkf_acc[here, :] = dkf
                dvf_acc[here, :] = dvf
            dqt = dot_nn(kn_t[rows, here], ds_near) + dot_nn(kf_t[rows, here], ds_far)
            for other in range(tile):
                there = slice(other * TILE, (other + 1) * TILE)
                prob = jnp.exp2(dot_nt(kf_ref[there, :], mine) - lse)
                dprob = dot_nt(vf_ref[there, :], grad_mine)
                dscore = (prob * (dprob - delta)).astype(low)
                dkf_acc[there, :] += dot_nn(dscore, mine)
                dvf_acc[there, :] += dot_nn(prob.astype(low), grad_mine)
                dqt = dqt + dot_nn(kf_t[rows, there], dscore)
            dqt_acc[rows, :] = dqt
        dq = dqt_acc[...].T * (1.0 / math.sqrt(HEAD))
        dq = rotate_back(dq, cosine[here], sa[here], sb[here])
        dq_ref[here, :] = dq.astype(low)
        sum_q = sum_q + jnp.sum(dq, axis=0, keepdims=True)
        dkn = rotate_back(dkn * ln2, cosine[here], sa[here], sb[here])
        dkn_ref[here, :] = dkn.astype(low)
        sum_kn = sum_kn + jnp.sum(dkn, axis=0, keepdims=True)
        dvn_ref[here, :] = dvn.astype(low)
        sum_vn = sum_vn + jnp.sum(dvn, axis=0, keepdims=True)
    dkf = rotate_back(dkf_acc[...] * ln2, cosine, sa, sb)
    dvf = dvf_acc[...]
    dkf_ref[...] = dkf.astype(low)
    dvf_ref[...] = dvf.astype(low)
    sums_ref[0, 0:1, :] = sum_q
    sums_ref[0, 1:2, :] = sum_kn + jnp.sum(dkf, axis=0, keepdims=True)
    sums_ref[0, 2:3, :] = sum_vn + jnp.sum(dvf, axis=0, keepdims=True)


def attend_back(krow, qcol, q, kn, vn, kf, vf, do, o, lse, tables):
    count, width = q.shape
    pairs = width // PAIR
    pair_spec = pl.BlockSpec((count, PAIR), lambda p: (0, p))
    row = jax.ShapeDtypeStruct((count, width), low)
    return pl.pallas_call(
        attend_back_kernel,
        grid=(pairs,),
        in_specs=[whole_spec(krow.shape), whole_spec(qcol.shape)]
        + [pair_spec] * 7
        + [pl.BlockSpec((1, 2, count), lambda p: (p, 0, 0))]
        + [whole_spec(t.shape) for t in tables],
        out_specs=[pair_spec] * 5 + [pl.BlockSpec((1, 3, PAIR), lambda p: (p, 0, 0))],
        out_shape=[row] * 5 + [jax.ShapeDtypeStruct((pairs, 3, PAIR), wide)],
        scratch_shapes=[
            pltpu.VMEM((PAIR, TILE), wide),
            pltpu.VMEM((count, PAIR), wide),
            pltpu.VMEM((count, PAIR), wide),
        ],
        compiler_params=params(48),
        cost_estimate=cost(50e9, 20e6, 6e6),
        name="attend_back",
    )(krow, qcol, q, kn, vn, kf, vf, do, o, lse, *tables)


def outer_qkv_kernel(h_ref, hf_ref, dq_ref, dk_ref, dv_ref, dkf_ref, dvf_ref, out_ref):
    width = dq_ref.shape[1]
    own, clean = h_ref[...], hf_ref[...]
    out_ref[:, :width] = dot_tn(own, dq_ref[...]).astype(low)
    out_ref[:, width : 2 * width] = (
        dot_tn(own, dk_ref[...]) + dot_tn(clean, dkf_ref[...])
    ).astype(low)
    out_ref[:, 2 * width :] = (
        dot_tn(own, dv_ref[...]) + dot_tn(clean, dvf_ref[...])
    ).astype(low)


def outer_qkv(h, hf, dq, dk, dv, dkf, dvf, tile=256):
    count, width = h.shape
    return pl.pallas_call(
        outer_qkv_kernel,
        grid=(width // tile,),
        in_specs=[pl.BlockSpec((count, tile), lambda i: (0, i))] * 2
        + [whole_spec((count, width))] * 5,
        out_specs=pl.BlockSpec((tile, 3 * width), lambda i: (i, 0)),
        out_shape=jax.ShapeDtypeStruct((width, 3 * width), low),
        compiler_params=params(48),
        cost_estimate=cost(10 * count * width * width, 16e6),
        name="outer_qkv",
    )(h, hf, dq, dk, dv, dkf, dvf)


def project_back_kernel(noisy_ref, x_ref, far_ref, dy_ref, dq_ref, dk_ref, dv_ref, dkf_ref,
                        dvf_ref, w_ref, gain1_ref, dx_ref, dfar_ref, gain1g_ref, bias1g_ref):
    width = x_ref.shape[1]

    @pl.when(pl.program_id(0) == 0)
    def _():
        for ref in (gain1g_ref, bias1g_ref):
            ref[...] = jnp.zeros_like(ref)

    parts = [w_ref[:, i * width : (i + 1) * width] for i in range(3)]
    noisy = noisy_ref[0] == 1
    own = x_ref[...].astype(wide)
    source = jnp.where(noisy, far_ref[...].astype(wide), own)
    normed, factor = normalize(own)
    normed_far, factor_far = normalize(source)
    dh = dot_nt(dq_ref[...], parts[0]) + dot_nt(dk_ref[...], parts[1]) + dot_nt(
        dv_ref[...], parts[2]
    )
    dh_far = dot_nt(dkf_ref[...], parts[1]) + dot_nt(dvf_ref[...], parts[2])
    gain1g_ref[...] += jnp.sum(dh * normed + dh_far * normed_far, axis=0, keepdims=True)
    bias1g_ref[...] += jnp.sum(dh + dh_far, axis=0, keepdims=True)
    gain = gain1_ref[...]
    dx = dy_ref[...] + norm_back(dh * gain, normed, factor)
    dfar = norm_back(dh_far * gain, normed_far, factor_far)
    dx_ref[...] = dx + jnp.where(noisy, 0.0, dfar)
    dfar_ref[...] = dfar.astype(low)


def project_back(noisy, x, far, dy, dq, dk, dv, dkf, dvf, weight, gain1):
    count, width = x.shape
    vec = jax.ShapeDtypeStruct((1, width), wide)
    return pl.pallas_call(
        project_back_kernel,
        grid=(count // ROWS,),
        in_specs=[pl.BlockSpec(memory_space=pltpu.SMEM)]
        + [row_spec(width)] * 8
        + [whole_spec(weight.shape), whole_spec(gain1.shape)],
        out_specs=[row_spec(width), row_spec(width), whole_spec((1, width)), whole_spec((1, width))],
        out_shape=[
            jax.ShapeDtypeStruct((count, width), wide),
            jax.ShapeDtypeStruct((count, width), low),
            vec,
            vec,
        ],
        compiler_params=params(48),
        cost_estimate=cost(10 * count * width * width, 24e6),
        name="project_back",
    )(noisy, x, far, dy, dq, dk, dv, dkf, dvf, weight, gain1)


def reduce_rows(part):
    part = lax.psum_scatter(part, "batch", scatter_dimension=0, tiled=True)
    return lax.psum(part, "stream").astype(wide)


def reduce_vectors(vectors, batch):
    packed = jnp.concatenate([v.reshape(batch, -1) for v in vectors], axis=1)
    width = packed.shape[1]
    padded = jnp.pad(packed, ((0, 0), (0, -width % 128)))
    summed = lax.psum_scatter(padded, "batch", scatter_dimension=0, tiled=True)
    summed = lax.psum(summed, "stream")[0]
    sizes = [v.size // batch for v in vectors]
    starts = [sum(sizes[:i]) for i in range(len(sizes))]
    return [summed[s : s + n] for s, n in zip(starts, sizes)]


def local(
    layer_input,
    out_cotangent,
    block_size,
    norm1_gain,
    norm1_bias,
    qkv_weight,
    qkv_bias,
    proj_weight,
    proj_bias,
    norm2_gain,
    norm2_bias,
    up_weight,
    up_bias,
    down_weight,
    down_bias,
):
    length, width = layer_input.shape[2:]
    batch = lax.axis_size("batch")
    noisy = lax.axis_index("stream").astype(jnp.int32).reshape(1)
    x = layer_input.reshape(length, width)
    g = out_cotangent.reshape(length, width)
    far_x = lax.ppermute(x, "stream", [(0, 1)])
    tables = rotary_tables(length)
    qkv_bias, norm1_gain, norm1_bias, proj_bias, norm2_gain, norm2_bias, up_bias, down_bias = (
        v.reshape(1, -1)
        for v in (
            qkv_bias,
            norm1_gain,
            norm1_bias,
            proj_bias,
            norm2_gain,
            norm2_bias,
            up_bias,
            down_bias,
        )
    )
    places = jnp.arange(TILE, dtype=jnp.int32) // block_size[0]
    krow, qcol = places[:, None], places[None, :]
    h, q, k, v = project(x, qkv_weight, qkv_bias, norm1_gain, norm1_bias, tables)
    hf, kf, vf = project_far(
        noisy, x, far_x, qkv_weight, qkv_bias, norm1_gain, norm1_bias, tables
    )
    o, lse = attend(krow, qcol, q, k, v, kf, vf)
    (
        out,
        h2,
        a,
        du,
        dy,
        dy_low,
        do,
        downb_grad,
        upb_grad,
        gain2_grad,
        bias2_grad,
        projb_grad,
    ) = middle(
        x,
        o,
        g,
        proj_weight,
        proj_bias,
        norm2_gain,
        norm2_bias,
        up_weight,
        up_bias,
        down_weight,
        down_bias,
    )
    downw = outer(a, g)
    upw = outer(h2, du)
    projw = outer(o, dy_low)
    dq, dk, dv, dkf, dvf, sums = attend_back(krow, qcol, q, k, v, kf, vf, do, o, lse, tables)
    qkvb_grad = sums.transpose(1, 0, 2).reshape(1, -1)
    qkvw = outer_qkv(h, hf, dq, dk, dv, dkf, dvf)
    dx, dfar, gain1_grad, bias1_grad = project_back(
        noisy, x, far_x, dy, dq, dk, dv, dkf, dvf, qkv_weight, norm1_gain
    )
    input_grad = (dx + lax.ppermute(dfar, "stream", [(1, 0)]).astype(wide)).reshape(
        layer_input.shape
    )
    downw_grad, upw_grad, projw_grad, qkvw_grad = (
        reduce_rows(part) for part in (downw, upw, projw, qkvw)
    )
    (
        gain1_grad,
        bias1_grad,
        qkvb_grad,
        projb_grad,
        gain2_grad,
        bias2_grad,
        upb_grad,
        downb_grad,
    ) = reduce_vectors(
        (
            gain1_grad,
            bias1_grad,
            qkvb_grad,
            projb_grad,
            gain2_grad,
            bias2_grad,
            upb_grad,
            downb_grad,
        ),
        batch,
    )
    return (
        out.reshape(layer_input.shape),
        input_grad,
        gain1_grad,
        bias1_grad,
        qkvw_grad,
        qkvb_grad,
        projw_grad,
        projb_grad,
        gain2_grad,
        bias2_grad,
        upw_grad,
        upb_grad,
        downw_grad,
        downb_grad,
    )


def solution(mesh):
    rows = P("stream", "batch", None, None)
    return jax.shard_map(
        local,
        mesh=mesh,
        in_specs=(rows, rows, P("batch")) + (P(),) * 12,
        out_specs=(
            rows,
            rows,
            P("batch"),
            P("batch"),
            P("batch", None),
            P("batch"),
            P("batch", None),
            P("batch"),
            P("batch"),
            P("batch"),
            P("batch", None),
            P("batch"),
            P("batch", None),
            P("batch"),
        ),
        check_vma=False,
    )
```

time: 1260 us -> 492 us (0.39)
  waiting for transfers between devices: 504 us -> 202 us
  matrix products: 240 us -> 0 us
  other arithmetic: 199 us -> 11.2 us
  Pallas kernels: 0 us -> 164 us
  local copies, waits for them, and re-layouts: 165 us -> 29.3 us
  loops' own time: 40.9 us -> 0 us
    ppermute x4 -> x2, waiting for transfers between devices: 311 us -> 13.6 us  [the longest x1 13.6 us: local(): far_x = lax.ppermute(x, 'stream', [(0, 1)])]
    dot_general x26 -> x0, matrix products: 240 us -> none  [the longest x4 40 us: times_transpose(): lax.dot_general(left, right, (((1,), (1,)), ((), ())), preferred_element_...]
    pallas_call x0 -> x10, Pallas kernels: none -> 164 us  [the longest x1 45 us: attend_back(): pl.pallas_call(attend_back_kernel, grid=(pairs,), in_specs=[whole_spec(kr...]
    convert_element_type x21 -> x4, other arithmetic: 76.4 us -> 5.14 us  [reduce_rows(): return lax.psum(part, 'stream').astype(wide)]
    another operation x21 -> x1, local copies, waits for them, and re-layouts: 51.7 us -> 0.09 us  [reduce_vectors(): packed = jnp.concatenate([v.reshape(batch, -1) for v in vectors], axis=1)]
    another operation x4 -> x0, loops' own time: 40.9 us -> none  [the longest x2 26.9 us: sequence_backward(): lax.cond(noisy, noisy_side, clean_side, 0)]
    reduce_sum x9 -> x0, other arithmetic: 34.4 us -> none  [the longest x2 15.5 us: clean_forward(): jnp.sum(jnp.exp(scores - top[..., None]), axis=-1)]
    psum x1, waiting for transfers between devices: 28.2 us -> 0.01 us  [reduce_rows(): return lax.psum(part, 'stream').astype(wide)]
  transfers between devices with their start and end apart: 9 -> 7, of which waited for: 7 -> 4; matrix products, arithmetic and copies ran while one was open for 16% -> 3% of each run, Pallas kernels for 0% -> 20%
where the time goes in v1:
time: 492 us; the launch traced here: 491 us
  waiting for transfers between devices  202 us (41%)
  Pallas kernels  164 us (33%)
  blocking collectives  63.1 us (13%)
  local copies, waits for them, and re-layouts  29.3 us (6%)
  between operations  14.7 us (3%)
  other arithmetic  11.2 us (2%)
  starting transfers between devices  6.46 us (1%)
    reduce_scatter x4, waiting for transfers between devices, reduce_rows(): part = lax.psum_scatter(part, 'batch', scatter_dimension=0, tiled=True)  189 us
    unnamed x1, blocking collectives  58.1 us
    pallas_call x1, Pallas kernels, attend_back(): pl.pallas_call(attend_back_kernel, grid=(pairs,), in_specs=[whole_spec(kr...  45 us
    pallas_call x1, Pallas kernels, middle(): pl.pallas_call(middle_kernel, grid=(count // ROWS,), in_specs=[row_spec(w...  35 us
    pallas_call x3, Pallas kernels, outer(): pl.pallas_call(outer_kernel, grid=(tall // tile,), in_specs=[pl.BlockSpec...  24.8 us
    pallas_call x1, Pallas kernels, attend(): pl.pallas_call(attend_kernel, grid=(pairs,), in_specs=[whole_spec(krow.sh...  24 us
    unnamed x62, local copies, waits for them, and re-layouts  21.5 us
    pallas_call x1, Pallas kernels, project_back(): pl.pallas_call(project_back_kernel, grid=(count // ROWS,), in_specs=[pl.B...  14 us
  transfers between devices with their start and end apart: 7, of which 4 were waited for; matrix products, arithmetic and copies ran while one was open for 3% of the time, Pallas kernels for 20%

profile of v1, /device:TPU:0, one launch (start us, length us, event | category | flops | bytes accessed | tf_op | source)
XLA Modules:
  0.0 490.7 jit_solution(9054424683349865254)
XLA Ops:
  7.2 5.0 %collective-permute-start = (bf16[1024,768]{1,0:T(8,128)(2,1)}, bf16[1024,768]{1,0:T(8,128)(2,1)S(1)}, u32[]{:S(2)}, u32[]{:S(2)}) collective-permute-start(bf16[1024,768]{1,0:T(8,128)(2,1)} %bitcast.27), channel_id=1, source_target_pairs={{0,16},{1,17},{2,18},{3,19},{4,20},{5,21},{6,22},{7,23},{8,24},{9,... | collective-permute-start | bytes 4718600 | tf_op jit(solution)/shard_map/ppermute | solution.py:580
  12.2 0.7 reshape.166.gain1_ref
  12.9 0.7 reshape.165.bias_ref
  13.6 0.7 reshape.167.bias1_ref
  15.0 0.7 reshape.170.bp_ref
  15.7 0.7 reshape.171.gain2_ref
  16.3 0.7 reshape.172.bias2_ref
  17.0 0.7 reshape.174.bd_ref
  17.7 0.1 and_select_fusion.qcol_ref
  17.8 1.3 add_select_fusion.krow_ref
  19.2 2.0 copy-done
  21.1 1.4 copy-done.1
  22.6 1.0 copy-done.3
  23.6 1.0 copy-done.5
  24.6 1.0 copy-done.7
  25.7 5.6 %project.1 = (bf16[1024,768]{1,0:T(8,128)(2,1)S(1)}, bf16[1024,768]{1,0:T(8,128)(2,1)S(1)}, bf16[1024,768]{1,0:T(8,128)(2,1)S(1)}, bf16[1024,768]{1,0:T(8,128)(2,1)S(1)}) custom-call(bf16[1024,768]{1,0:T(8,128)(2,1)S(1)} %bitcast.29, bf16[768,2304]{1,0:T(8,128)(2,1)S(1)} %copy-done, f32[1,2304]{1,0:T(1,128)S(1)} %reshape.165.bias_ref, ...), custom_call_target="tpu_custom_call" | custom-call | flops 3623878656 | bytes 16000000 | tf_op jit(solution)/shard_map/project/pallas_call | solution.py:140
  31.3 1.1 copy-done.22
  32.5 13.6 %collective-permute-done.far_ref = bf16[1024,768]{1,0:T(8,128)(2,1)S(1)} collective-permute-done((bf16[1024,768]{1,0:T(8,128)(2,1)}, bf16[1024,768]{1,0:T(8,128)(2,1)S(1)}, u32[]{:S(2)}, u32[]{:S(2)}) %collective-permute-start) | collective-permute-done | bytes 1572896 | tf_op jit(solution)/shard_map/ppermute | solution.py:580
  46.1 4.4 project_far.1
  50.4 1.2 copy-done.10
  51.6 1.2 copy-done.12
  52.8 1.2 copy-done.13
  54.0 24.0 %attend.1 = (bf16[1024,768]{1,0:T(8,128)(2,1)S(1)}, f32[6,2,1024]{2,1,0:T(2,128)S(1)}) custom-call(s32[256,1]{1,0:T(8,128)S(1)} %add_select_fusion.krow_ref, s32[1,256]{1,0:T(1,128)S(1)} %and_select_fusion.qcol_ref, bf16[1024,768]{1,0:T(8,128)(2,1)S(1)} %get-tuple-element.45.q_ref, bf16[1024,768]{1,0:T(8,128)(2,1)S(1)} %get-tuple-element.46.kn_ref, ...), custom_call_target="tpu_custom_call" | custom-call | flops 20000000000 | bytes 10000000 | tf_op jit(solution)/shard_map/attend/pallas_call | solution.py:233
  78.0 1.2 copy-done.16
  79.2 35.0 %middle.1 = (bf16[1024,768]{1,0:T(8,128)(2,1)}, bf16[1024,768]{1,0:T(8,128)(2,1)}, bf16[1024,3072]{1,0:T(8,128)(2,1)}, bf16[1024,3072]{1,0:T(8,128)(2,1)}, f32[1...) custom-call(bf16[1024,768]{1,0:T(8,128)(2,1)} %bitcast.28, ...), custom_call_target="tpu_custom_call" | custom-call | flops 21743271936 | bytes 40000000 | tf_op jit(solution)/shard_map/middle/pallas_call | solution.py:301
  114.2 1.4 copy-done.18
  115.6 2.8 outer.3
  118.6 45.0 %attend_back.1 = (bf16[1024,768]{1,0:T(8,128)(2,1)S(1)}, bf16[1024,768]{1,0:T(8,128)(2,1)S(1)}, bf16[1024,768]{1,0:T(8,128)(2,1)}, bf16[1024,768]{1,0:T(8,128)(2...) custom-call(s32[256,1]{1,0:T(8,128)S(1)} %add_select_fusion.krow_ref, s32[1,256]{1,0:T(1,128)S(1)} %and_select_fusion.qcol_ref, ...), custom_call_target="tpu_custom_call" | custom-call | flops 49999998976 | bytes 20000000 | tf_op jit(solution)/shard_map/attend_back/pallas_call | solution.py:445
  163.5 1.1 copy-done.20
  164.7 10.9 %outer_qkv.1 = bf16[768,2304]{1,0:T(8,128)(2,1)} custom-call(bf16[1024,768]{1,0:T(8,128)(2,1)S(1)} %copy-done.23, bf16[1024,768]{1,0:T(8,128)(2,1)S(1)} %copy-done.11, bf16[1024,768]{1,0:T(8,128)(2,1)S(1)} %get-tuple-element.55.dq_ref, bf16[1024,768]{1,0:T(8,128)(2,1)} %copy-done.20, bf16[1024,768]{1,0:T(8,128)(2,1)} %get-tuple-element.57.dv_ref, ...), custom_call_target="tpu_custom_call" | custom-call | flops 6039797760 | bytes 16000000 | tf_op jit(solution)/shard_map/outer_qkv/pallas_call | solution.py:479
  175.6 1.2 copy-done.19
  176.9 1.3 copy-done.21
  178.2 9.5 %outer.4 = bf16[768,3072]{1,0:T(8,128)(2,1)} custom-call(bf16[1024,768]{1,0:T(8,128)(2,1)S(1)} %copy-done.21, bf16[1024,3072]{1,0:T(8,128)(2,1)} %get-tuple-element.74.right_ref), custom_call_target="tpu_custom_call" | custom-call | flops 4831838208 | bytes 12582912 | tf_op jit(solution)/shard_map/outer/pallas_call | solution.py:343
  187.8 1.4 copy-done.9
  189.2 12.5 %outer.5 = bf16[3072,768]{1,0:T(8,128)(2,1)} custom-call(bf16[1024,3072]{1,0:T(8,128)(2,1)} %get-tuple-element.75.left_ref, bf16[1024,768]{1,0:T(8,128)(2,1)S(1)} %bitcast.34), custom_call_target="tpu_custom_call" | custom-call | flops 4831838208 | bytes 12582912 | tf_op jit(solution)/shard_map/outer/pallas_call | solution.py:343
  201.8 1.3 copy-done.2
  203.1 14.0 %project_back.1 = (f32[1024,768]{1,0:T(8,128)}, bf16[1024,768]{1,0:T(8,128)(2,1)}, f32[1,768]{1,0:T(1,128)S(1)}, f32[1,768]{1,0:T(1,128)S(1)}) custom-call(s32[1]{0:T(128)} %bitcast.2.noisy_ref, bf16[1024,768]{1,0:T(8,128)(2,1)S(1)} %bitcast.31, bf16[1024,768]{1,0:T(8,128)(2,1)S(1)} %collective-permute-done.far_ref, f32[1024,768]{1,0:T(8,128)} %get-tuple-element.52.dy_ref, ...), custom_call_target="tpu_custom_call" | custom-call | flops 6039797760 | bytes 24000000 | tf_op jit(solution)/shard_map/project_back/pallas_call | solution.py:523
  217.1 1.3 collective-permute-start.1
  218.4 31.4 %reduce-scatter.5.cloned.1.call-done = bf16[48,2304]{1,0:T(8,128)(2,1)} async-done(((bf16[768,2304]{1,0:T(8,128)(2,1)}), bf16[48,2304]{1,0:T(8,128)(2,1)}) %reduce-scatter.5.cloned.1.call-update) | async-done | bytes 221200 | tf_op jit(solution)/shard_map/reduce_scatter | solution.py:543
  249.8 78.3 %reduce-scatter.9.cloned.1.call-done = bf16[48,3072]{1,0:T(8,128)(2,1)} async-done(((bf16[768,3072]{1,0:T(8,128)(2,1)}), bf16[48,3072]{1,0:T(8,128)(2,1)}) %reduce-scatter.9.cloned.1.call-update) | async-done | bytes 294928 | tf_op jit(solution)/shard_map/reduce_scatter | solution.py:543
  328.2 78.8 %reduce-scatter.11.cloned.1.call-done = bf16[192,768]{1,0:T(8,128)(2,1)} async-done(((bf16[3072,768]{1,0:T(8,128)(2,1)}), bf16[192,768]{1,0:T(8,128)(2,1)}) %reduce-scatter.11.cloned.1.call-update) | async-done | bytes 294928 | tf_op jit(solution)/shard_map/reduce_scatter | solution.py:543
  407.0 0.6 dynamic-slice
  407.6 0.1 reshape.177
  407.7 0.1 reshape.178
  407.8 0.1 reshape_reshape.3
  407.9 0.5 broadcast.82
  408.4 0.7 reduce.9
  409.1 0.1 reshape.182
  409.2 0.1 reshape.179
  409.3 0.1 reshape.180
  409.4 0.1 reshape.181
  409.5 0.1 reshape.183
  409.5 0.1 concatenate.3
  409.6 58.1 %all-reduce.1 = f32[16,640]{1,0:T(8,128)S(1)} all-reduce(f32[16,640]{1,0:T(8,128)S(1)} %pad.4), channel_id=2, replica_groups=mesh['stream'=2,'batch'=16] {'batch'}, use_global_device_ids=true, to_apply=%region_0.1.clone | all-reduce | flops 10240 | bytes 81920
  467.8 0.7 constant_dynamic-slice_fusion
  468.4 4.9 %psum.35 = f32[1,640]{1,0:T(1,128)S(1)} all-reduce(f32[1,640]{1,0:T(1,128)S(1)} %constant_dynamic-slice_fusion), channel_id=1, replica_groups=mesh['stream'=2,'batch'=16] {'stream'}, use_global_device_ids=true, to_apply=%region_1.2 | all-reduce | flops 640 | bytes 5120 | tf_op jit(solution)/shard_map/psum | solution.py:552
  473.4 0.6 slice.66
  474.0 0.6 slice.70
  474.6 0.6 slice_bitcast_fusion
  475.2 3.9 add_bitcast_fusion
  479.0 1.9 convert_element_type.20
  480.9 1.8 convert_element_type.21
  482.7 0.8 convert_element_type.18
  483.5 0.7 convert_element_type.19
  (65 shorter events, 0.5 us)
Async XLA Ops:
  7.2 211.2 %reduce-scatter.7.cloned.1.call-start = ((), (), s32[]{:S(2)}) async-start(), calls=%async_computation.5 | async-start | bytes 1253376 | tf_op jit(solution)/shard_map/reduce_scatter | solution.py:543
  7.2 38.8 %collective-permute-start = (bf16[1024,768]{1,0:T(8,128)(2,1)}, bf16[1024,768]{1,0:T(8,128)(2,1)S(1)}, u32[]{:S(2)}, u32[]{:S(2)}) collective-permute-start(bf16[1024,768]{1,0:T(8,128)(2,1)} %bitcast.27), channel_id=1, source_target_pairs={{0,16},{1,17},{2,18},{3,19},{4,20},{5,21},{6,22},{7,23},{8,24},{9,... | collective-permute-start | bytes 4718600 | tf_op jit(solution)/shard_map/ppermute | solution.py:580
  19.1 2.0 copy-start
  21.1 1.4 copy-start.1
  22.6 1.0 copy-start.3
  23.6 1.0 copy-start.5
  24.6 1.0 copy-start.7
  31.3 1.1 copy-start.22
  32.5 17.9 %copy-start.26 = (bf16[1024,768]{1,0:T(8,128)(2,1)}, bf16[1024,768]{1,0:T(8,128)(2,1)S(1)}, u32[]{:S(2)}) copy-start(bf16[1024,768]{1,0:T(8,128)(2,1)S(1)} %get-tuple-element.47.vn_ref) | copy-start | bytes 4718596
  32.5 21.5 %copy-start.24 = (bf16[1024,768]{1,0:T(8,128)(2,1)}, bf16[1024,768]{1,0:T(8,128)(2,1)S(1)}, u32[]{:S(2)}) copy-start(bf16[1024,768]{1,0:T(8,128)(2,1)S(1)} %get-tuple-element.45.q_ref) | copy-start | bytes 4718596
  32.5 21.5 %copy-start.25 = (bf16[1024,768]{1,0:T(8,128)(2,1)}, bf16[1024,768]{1,0:T(8,128)(2,1)S(1)}, u32[]{:S(2)}) copy-start(bf16[1024,768]{1,0:T(8,128)(2,1)S(1)} %get-tuple-element.46.kn_ref) | copy-start | bytes 4718596
  50.4 1.2 copy-start.10
  51.6 1.2 copy-start.12
  52.8 1.2 copy-start.13
  54.0 25.2 %copy-start.14 = (bf16[768,768]{1,0:T(8,128)(2,1)S(1)}, bf16[768,768]{1,0:T(8,128)(2,1)}, u32[]{:S(2)}) copy-start(bf16[768,768]{1,0:T(8,128)(2,1)} %wp_ref.1) | copy-start | bytes 3538948
  54.0 25.2 %copy-start.15 = (f32[3072]{0:T(1024)S(1)}, f32[3072]{0:T(1024)}, u32[]{:S(2)}) copy-start(f32[3072]{0:T(1024)} %param.30) | copy-start | bytes 36868
  78.0 1.2 copy-start.16
  79.2 35.0 %copy-start.17 = (bf16[1024,768]{1,0:T(8,128)(2,1)S(1)}, bf16[1024,768]{1,0:T(8,128)(2,1)}, u32[]{:S(2)}) copy-start(bf16[1024,768]{1,0:T(8,128)(2,1)} %copy-done.16) | copy-start | bytes 4718596
  114.2 1.4 copy-start.18
  115.6 2.9 copy-start.4
  115.6 2.9 copy-start.6
  115.6 2.9 copy-start.8
  118.5 131.3 %reduce-scatter.5.cloned.1.call-start = ((), (), s32[]{:S(2)}) async-start(), calls=%async_computation.4 | async-start | bytes 3760128 | tf_op jit(solution)/shard_map/reduce_scatter | solution.py:543
  118.6 46.1 %copy-start.11 = (bf16[1024,768]{1,0:T(8,128)(2,1)S(1)}, bf16[1024,768]{1,0:T(8,128)(2,1)}, u32[]{:S(2)}) copy-start(bf16[1024,768]{1,0:T(8,128)(2,1)} %copy-done.10) | copy-start | bytes 4718596
  118.6 46.1 %copy-start.23 = (bf16[1024,768]{1,0:T(8,128)(2,1)S(1)}, bf16[1024,768]{1,0:T(8,128)(2,1)}, u32[]{:S(2)}) copy-start(bf16[1024,768]{1,0:T(8,128)(2,1)} %copy-done.22) | copy-start | bytes 4718596
  163.5 1.2 copy-start.20
  175.6 1.2 copy-start.19
  176.8 1.4 copy-start.21
  176.8 151.3 %reduce-scatter.9.cloned.1.call-start = ((), (), s32[]{:S(2)}) async-start(), calls=%async_computation.6 | async-start | bytes 5013504 | tf_op jit(solution)/shard_map/reduce_scatter | solution.py:543
  187.7 1.5 copy-start.9
  187.8 219.2 %reduce-scatter.11.cloned.1.call-start = ((), (), s32[]{:S(2)}) async-start(), calls=%async_computation.7 | async-start | bytes 5013504 | tf_op jit(solution)/shard_map/reduce_scatter | solution.py:543
  201.7 1.4 copy-start.2
  201.7 277.3 %all-reduce.5.cloned.1.call-start = ((), (), s32[]{:S(2)}) async-start(), calls=%async_computation.8 | async-start | bytes 1769472 | tf_op jit(solution)/shard_map/psum | solution.py:544
  203.1 203.9 %copy-start.29 = (u32[32]{0:T(128)S(1)}, u32[32]{0:T(128)}, u32[]{:S(2)}) copy-start(u32[32]{0:T(128)} %constant.32) | copy-start | bytes 388
  217.1 258.1 %collective-permute-start.1 = (bf16[1024,768]{1,0:T(8,128)(2,1)}, bf16[1024,768]{1,0:T(8,128)(2,1)S(1)}, u32[]{:S(2)}, u32[]{:S(2)}) collective-permute-start(bf16[1024,768]{1,0:T(8,128)(2,1)} %get-tuple-element.61), channel_id=1, source_target_pairs={{16,0},{17,1},{18,2},{19,3},{20,4},{21,5},{22,6},{23,7},{24,8},{25... | collective-permute-start | bytes 4718600 | tf_op jit(solution)/shard_map/ppermute | solution.py:637
  479.0 3.7 copy-start.27
  479.0 4.5 copy-start.28
Sparse Core Ops, SparseCore 0:
  118.6 60.1 reduce-scatter.6
  182.7 67.0 reduce-scatter.4
  253.7 74.4 reduce-scatter.8
  332.4 74.5 reduce-scatter.10
  409.3 36.1 all-reduce.4
